TPU v7x, 32 devices: a whole 2x2x4 slice. The times are simulated.
32 devices in a mesh: row: 4 (over y, x), col: 8 (over z, core).
Axes of the slice: x: 2, y: 2, z: 4, core: 2. Of those that a mesh axis runs over, the one named last changes fastest.
Arguments:
- density: bfloat16 [3072, 3072], P('row', 'col'), as said below
- pattern: int32 [2, 24, 24], P(None, 'row', 'col'), may hold values from 0 to 1, as said below
- kept_slots: int32 [2, 4, 8, 12], P(None, 'row', 'col'), may hold values from 0 to 17, as said below
- owner_shift: int32 [6], replicated, may hold values from 0 to 3
- owner_slot: int32 [4, 6], replicated, may hold values from 0 to 5, each once within a row
Outputs:
- purified: bfloat16 [3072, 3072], P('row', 'col')
- traces: float32 [2], replicated
Inputs may be any that keep to these rules, and one draw needn't show every extreme that they name: Symmetric, as a density matrix is. `kept_slots`: each device's 12 entries of one multiply are distinct. `pattern`: symmetric in its last two dimensions; every diagonal block is 1. `owner_slot`: each row is a permutation.
All inputs are finite; a program needn't handle non-finite values.
Results may differ from a plain program's by a relative error of at most 0.0047.
Values may be sent and summed in bfloat16 or wider, within the bound.
A program may use at most 64 MiB of HBM per device.

v0:
```python
import jax
import jax.numpy as jnp
from jax import lax
from jax.sharding import PartitionSpec as P


def passed_along(value, axis, steps):
    count = lax.axis_size(axis)
    pairs = [(source, (source + steps) % count) for source in range(count)]
    return lax.ppermute(value, axis, pairs)


def partner_2(block, axis, distance):
    count = lax.axis_size(axis)
    route = []
    for low in range(count):
        high = low | 1 << distance
        if high != low and high < count:
            route += [(low, high), (high, low)]
    return lax.ppermute(block, axis, route)


def shift_rows(value, steps):
    return passed_along(value, "row", steps)


def shift_cols(value, steps):
    return passed_along(value, "col", steps)


def partner(value):
    return partner_2(value, "col", 0)


def assemble(half, other, parity):
    return jnp.where(
        parity == 0, jnp.concatenate([half, other], axis=1), jnp.concatenate([other, half], axis=1)
    )


def skewed(operand, row_index, group):
    nrow = lax.axis_size("row")
    ncol = lax.axis_size("col")
    left = operand
    right = operand
    for bit in range(nrow.bit_length() - 1):
        moved = shift_cols(left, ncol - (2 << bit))
        left = jnp.where(row_index >> bit & 1 == 1, moved, left)
        moved = shift_rows(right, nrow - (1 << bit))
        right = jnp.where(group >> bit & 1 == 1, moved, right)
    return (left, right)


def multiply(tile, occupancy, kept, flipped, row_index, col_index):
    rows, cols = tile.shape
    nrb, ncb = occupancy.shape
    bdim = rows // nrb
    nrow = lax.axis_size("row")
    ncol = lax.axis_size("col")
    group = col_index // 2
    parity = col_index % 2
    operand = (
        tile.reshape(nrb, bdim, ncb, bdim) * occupancy[:, None, :, None].astype(tile.dtype)
    ).reshape(rows, cols)
    accum = jnp.zeros((rows, cols), jnp.float32)
    left, right = skewed(operand, row_index, group)
    for step in range(nrow):
        panel = assemble(left, partner(left), parity)
        accum = accum + jnp.dot(panel, right, preferred_element_type=jnp.float32)
        if step + 1 < nrow:
            left = shift_cols(left, ncol - 2)
            right = shift_rows(right, nrow - 1)
    if flipped:
        update = 2.0 * operand.astype(jnp.float32) - accum
    else:
        update = accum
    keepers = jnp.any(kept[:, None] == jnp.arange(nrb * ncb, dtype=jnp.int32)[None, :], axis=0)
    keepers = keepers.reshape(nrb, ncb).astype(jnp.float32)
    update = (update.reshape(nrb, bdim, ncb, bdim) * keepers[:, None, :, None]).reshape(rows, cols)
    return update.astype(jnp.bfloat16)


def local_trace(tile, row_index, col_index):
    rows, cols = tile.shape
    global_row = row_index * rows + jnp.arange(rows, dtype=jnp.int32)[:, None]
    global_col = col_index * cols + jnp.arange(cols, dtype=jnp.int32)[None, :]
    return jnp.sum(jnp.where(global_row == global_col, tile.astype(jnp.float32), 0.0))


def relabel(tile, shifts, slots, row_index, col_index):
    rows, cols = tile.shape
    nrb = shifts.shape[0]
    ncb = nrb // 2
    bdim = rows // nrb
    nrow = lax.axis_size("row")
    parity = col_index % 2
    col_local = parity * ncb + jnp.arange(ncb, dtype=jnp.int32)
    col_shift = shifts[col_local]
    for bit in range(nrow.bit_length() - 1):
        moved = shift_rows(tile, 1 << bit)
        take_rows = jnp.repeat(shifts >> bit & 1 == 1, bdim)
        tile = jnp.where(take_rows[:, None], moved, tile)
        moved = shift_cols(tile, 2 << bit)
        take_cols = jnp.repeat(col_shift >> bit & 1 == 1, bdim)
        tile = jnp.where(take_cols[None, :], moved, tile)
    inverse_rows = jnp.argsort(slots[row_index])
    inverse_cols = jnp.argsort(slots[col_index // 2])
    other = partner(tile)
    both = jnp.concatenate([tile.reshape(rows, ncb, bdim), other.reshape(rows, ncb, bdim)], axis=1)
    wanted = inverse_cols[parity * ncb + jnp.arange(ncb, dtype=jnp.int32)]
    pick = jnp.where(wanted // ncb == parity, 0, ncb) + wanted % ncb
    tile = jnp.take(both, pick, axis=1).reshape(rows, cols)
    return jnp.take(tile.reshape(nrb, bdim, cols), inverse_rows, axis=0).reshape(rows, cols)


def body(density, pattern, kept_slots, owner_shift, owner_slot):
    row_index = lax.axis_index("row")
    col_index = lax.axis_index("col")
    first = multiply(density, pattern[0], kept_slots[0, 0, 0], False, row_index, col_index)
    trace_one = local_trace(first, row_index, col_index)
    relabelled = relabel(first, owner_shift, owner_slot, row_index, col_index)
    second = multiply(relabelled, pattern[1], kept_slots[1, 0, 0], True, row_index, col_index)
    trace_two = local_trace(second, row_index, col_index)
    totals = lax.psum((trace_one, trace_two), ("row", "col"))
    return (second, jnp.stack([totals[0], totals[1]]))


def solution(mesh):
    placed = (P("row", "col"), P(None, "row", "col"), P(None, "row", "col", None), P(), P())
    return jax.shard_map(
        body, mesh=mesh, in_specs=placed, out_specs=(P("row", "col"), P()), check_vma=False
    )
```

profile of v0, /device:TPU:0, one launch (start us, length us, event | category | flops | bytes accessed | tf_op | source)
XLA Modules:
  0.0 323.7 jit_solution(17280223341478196376)
XLA Ops:
  2.9 5.1 %collective-permute-start = (bf16[768,384]{0,1:T(8,128)(2,1)S(1)}, bf16[768,384]{0,1:T(8,128)(2,1)S(1)}, u32[]{:S(2)}, u32[]{:S(2)}) collective-permute-start(bf16[768,384]{0,1:T(8,128)(2,1)S(1)} %bitcast_multiply_fusion.1), channel_id=1, source_target_pairs={{0,6},{1,7},{2,0},{3,1},{4,2},{5,3},{6,4},{7,5},{8,14},{9,15},{10,... | collective-permute-start | bytes 1769480 | tf_op jit(solution)/shard_map/ppermute | solution.py:10
  8.0 2.4 collective-permute-start.3
  10.5 10.1 %collective-permute-done = bf16[768,384]{0,1:T(8,128)(2,1)S(1)} collective-permute-done((bf16[768,384]{0,1:T(8,128)(2,1)S(1)}, bf16[768,384]{0,1:T(8,128)(2,1)S(1)}, u32[]{:S(2)}, u32[]{:S(2)}) %collective-permute-start) | collective-permute-done | bytes 589856 | tf_op jit(solution)/shard_map/ppermute | solution.py:10
  20.6 2.2 collective-permute-done.3
  24.6 25.6 %collective-permute-done.1 = bf16[768,384]{0,1:T(8,128)(2,1)S(1)} collective-permute-done((bf16[768,384]{0,1:T(8,128)(2,1)S(1)}, bf16[768,384]{0,1:T(8,128)(2,1)S(1)}, u32[]{:S(2)}, u32[]{:S(2)}) %collective-permute-start.1) | collective-permute-done | bytes 589856 | tf_op jit(solution)/shard_map/ppermute | solution.py:10
  51.8 3.4 %collective-permute-start.7 = (bf16[768,384]{0,1:T(8,128)(2,1)S(1)}, bf16[768,384]{0,1:T(8,128)(2,1)}, u32[]{:S(2)}, u32[]{:S(2)}) collective-permute-start(bf16[768,384]{0,1:T(8,128)(2,1)S(1)} %broadcast_select_fusion.5), channel_id=1, source_target_pairs={{0,24},{8,0},{16,8},{24,16},{1,25},{9,1},{17,9},{25,17},{2,26},{10... | collective-permute-start | bytes 1769480 | tf_op jit(solution)/shard_map/ppermute | solution.py:10
  55.2 10.4 %collective-permute-done.5 = bf16[768,384]{0,1:T(8,128)(2,1)S(1)} collective-permute-done((bf16[768,384]{0,1:T(8,128)(2,1)S(1)}, bf16[768,384]{0,1:T(8,128)(2,1)S(1)}, u32[]{:S(2)}, u32[]{:S(2)}) %collective-permute-start.5) | collective-permute-done | bytes 589856 | tf_op jit(solution)/shard_map/ppermute | solution.py:10
  65.5 3.2 collective-permute-start.8
  68.8 3.3 %collective-permute-start.10 = (bf16[768,384]{0,1:T(8,128)(2,1)}, bf16[768,384]{0,1:T(8,128)(2,1)}, u32[]{:S(2)}, u32[]{:S(2)}) collective-permute-start(bf16[768,384]{0,1:T(8,128)(2,1)} %collective-permute-done.7), channel_id=1, source_target_pairs={{0,24},{8,0},{16,8},{24,16},{1,25},{9,1},{17,9},{25,17},{2,26},{10... | collective-permute-start | bytes 1769480 | tf_op jit(solution)/shard_map/ppermute | solution.py:10
  72.6 8.1 %collective-permute-done.8 = bf16[768,384]{0,1:T(8,128)(2,1)} collective-permute-done((bf16[768,384]{0,1:T(8,128)(2,1)S(1)}, bf16[768,384]{0,1:T(8,128)(2,1)}, u32[]{:S(2)}, u32[]{:S(2)}) %collective-permute-start.8) | collective-permute-done | bytes 589856 | tf_op jit(solution)/shard_map/ppermute | solution.py:10
  80.7 4.4 %collective-permute-start.11 = (bf16[768,384]{0,1:T(8,128)(2,1)}, bf16[768,384]{0,1:T(8,128)(2,1)}, u32[]{:S(2)}, u32[]{:S(2)}) collective-permute-start(bf16[768,384]{0,1:T(8,128)(2,1)} %collective-permute-done.8), channel_id=1, source_target_pairs={{0,6},{1,7},{2,0},{3,1},{4,2},{5,3},{6,4},{7,5},{8,14},{9,15},{10,... | collective-permute-start | bytes 1769480 | tf_op jit(solution)/shard_map/ppermute | solution.py:10
  85.3 3.4 %collective-permute-start.13 = (bf16[768,384]{0,1:T(8,128)(2,1)}, bf16[768,384]{0,1:T(8,128)(2,1)S(1)}, u32[]{:S(2)}, u32[]{:S(2)}) collective-permute-start(bf16[768,384]{0,1:T(8,128)(2,1)} %collective-permute-done.10), channel_id=1, source_target_pairs={{0,24},{8,0},{16,8},{24,16},{1,25},{9,1},{17,9},{25,17},{2,26},{10... | collective-permute-start | bytes 1769480 | tf_op jit(solution)/shard_map/ppermute | solution.py:10
  88.7 2.1 fusion.12
  90.9 5.5 %collective-permute-done.11 = bf16[768,384]{0,1:T(8,128)(2,1)} collective-permute-done((bf16[768,384]{0,1:T(8,128)(2,1)}, bf16[768,384]{0,1:T(8,128)(2,1)}, u32[]{:S(2)}, u32[]{:S(2)}) %collective-permute-start.11) | collective-permute-done | bytes 589856 | tf_op jit(solution)/shard_map/ppermute | solution.py:10
  98.3 2.1 convolution_add_fusion.4
  102.5 2.1 fusion.3
  104.6 2.4 collective-permute-start.14
  108.0 13.1 %collective-permute-done.14 = bf16[768,384]{0,1:T(8,128)(2,1)S(1)} collective-permute-done((bf16[768,384]{0,1:T(8,128)(2,1)S(1)}, bf16[768,384]{0,1:T(8,128)(2,1)S(1)}, u32[]{:S(2)}, u32[]{:S(2)}) %collective-permute-start.14) | collective-permute-done | bytes 589856 | tf_op jit(solution)/shard_map/ppermute | solution.py:10
  122.0 16.1 %collective-permute-done.15 = bf16[768,384]{0,1:T(8,128)(2,1)S(1)} collective-permute-done((bf16[768,384]{0,1:T(8,128)(2,1)S(1)}, bf16[768,384]{0,1:T(8,128)(2,1)S(1)}, u32[]{:S(2)}, u32[]{:S(2)}) %collective-permute-start.15) | collective-permute-done | bytes 589856 | tf_op jit(solution)/shard_map/ppermute | solution.py:10
  140.6 11.8 %collective-permute-done.16 = bf16[768,384]{0,1:T(8,128)(2,1)S(1)} collective-permute-done((bf16[768,384]{0,1:T(8,128)(2,1)S(1)}, bf16[768,384]{0,1:T(8,128)(2,1)S(1)}, u32[]{:S(2)}, u32[]{:S(2)}) %collective-permute-start.16) | collective-permute-done | bytes 589856 | tf_op jit(solution)/shard_map/ppermute | solution.py:10
  152.7 26.1 %collective-permute-done.17 = bf16[768,384]{0,1:T(8,128)(2,1)S(1)} collective-permute-done((bf16[768,384]{0,1:T(8,128)(2,1)S(1)}, bf16[768,384]{0,1:T(8,128)(2,1)S(1)}, u32[]{:S(2)}, u32[]{:S(2)}) %collective-permute-start.17) | collective-permute-done | bytes 589856 | tf_op jit(solution)/shard_map/ppermute | solution.py:10
  187.0 12.5 %collective-permute-done.19 = bf16[768,384]{0,1:T(8,128)(2,1)S(1)} collective-permute-done((bf16[768,384]{0,1:T(8,128)(2,1)S(1)}, bf16[768,384]{0,1:T(8,128)(2,1)S(1)}, u32[]{:S(2)}, u32[]{:S(2)}) %collective-permute-start.19) | collective-permute-done | bytes 589856 | tf_op jit(solution)/shard_map/ppermute | solution.py:10
  201.5 27.2 %collective-permute-done.20 = bf16[768,384]{0,1:T(8,128)(2,1)S(1)} collective-permute-done((bf16[768,384]{0,1:T(8,128)(2,1)S(1)}, bf16[768,384]{0,1:T(8,128)(2,1)S(1)}, u32[]{:S(2)}, u32[]{:S(2)}) %collective-permute-start.20) | collective-permute-done | bytes 589856 | tf_op jit(solution)/shard_map/ppermute | solution.py:10
  230.3 2.0 collective-permute-start.26
  232.3 11.8 %collective-permute-done.24 = bf16[768,384]{0,1:T(8,128)(2,1)} collective-permute-done((bf16[768,384]{0,1:T(8,128)(2,1)S(1)}, bf16[768,384]{0,1:T(8,128)(2,1)}, u32[]{:S(2)}, u32[]{:S(2)}) %collective-permute-start.24) | collective-permute-done | bytes 589856 | tf_op jit(solution)/shard_map/ppermute | solution.py:10
  244.2 3.2 collective-permute-start.27
  249.4 10.3 %collective-permute-done.27 = bf16[768,384]{0,1:T(8,128)(2,1)S(1)} collective-permute-done((bf16[768,384]{0,1:T(8,128)(2,1)}, bf16[768,384]{0,1:T(8,128)(2,1)S(1)}, u32[]{:S(2)}, u32[]{:S(2)}) %collective-permute-start.27) | collective-permute-done | bytes 589856 | tf_op jit(solution)/shard_map/ppermute | solution.py:10
  259.6 4.2 %collective-permute-start.30 = (bf16[768,384]{0,1:T(8,128)(2,1)S(1)}, bf16[768,384]{0,1:T(8,128)(2,1)S(1)}, u32[]{:S(2)}, u32[]{:S(2)}) collective-permute-start(bf16[768,384]{0,1:T(8,128)(2,1)S(1)} %collective-permute-done.27), channel_id=1, source_target_pairs={{0,6},{1,7},{2,0},{3,1},{4,2},{5,3},{6,4},{7,5},{8,14},{9,15},{10,... | collective-permute-start | bytes 1769480 | tf_op jit(solution)/shard_map/ppermute | solution.py:10
  264.6 2.0 collective-permute-start.32
  266.5 2.4 fusion.33
  269.0 5.8 %collective-permute-done.30 = bf16[768,384]{0,1:T(8,128)(2,1)S(1)} collective-permute-done((bf16[768,384]{0,1:T(8,128)(2,1)S(1)}, bf16[768,384]{0,1:T(8,128)(2,1)S(1)}, u32[]{:S(2)}, u32[]{:S(2)}) %collective-permute-start.30) | collective-permute-done | bytes 589856 | tf_op jit(solution)/shard_map/ppermute | solution.py:10
  283.2 38.6 %all-reduce = (f32[1]{0:T(128)}, f32[1]{0:T(128)}) all-reduce(f32[1]{0:T(128)} %bitcast.20, f32[1]{0:T(128)} %bitcast.19), channel_id=1, replica_groups=mesh['row'=4,'col'=8] {'row','col'}, use_global_device_ids=true, to_apply=%region_7.8 | all-reduce | flops 2 | bytes 16 | tf_op jit(solution)/shard_map/psum | solution.py:124
  (110 shorter events, 39.7 us)
Async XLA Ops:
  2.9 17.7 %collective-permute-start = (bf16[768,384]{0,1:T(8,128)(2,1)S(1)}, bf16[768,384]{0,1:T(8,128)(2,1)S(1)}, u32[]{:S(2)}, u32[]{:S(2)}) collective-permute-start(bf16[768,384]{0,1:T(8,128)(2,1)S(1)} %bitcast_multiply_fusion.1), channel_id=1, source_target_pairs={{0,6},{1,7},{2,0},{3,1},{4,2},{5,3},{6,4},{7,5},{8,14},{9,15},{10,... | collective-permute-start | bytes 1769480 | tf_op jit(solution)/shard_map/ppermute | solution.py:10
  8.0 14.8 %collective-permute-start.3 = (bf16[768,384]{0,1:T(8,128)(2,1)S(1)}, bf16[768,384]{0,1:T(8,128)(2,1)S(1)}, u32[]{:S(2)}, u32[]{:S(2)}) collective-permute-start(bf16[768,384]{0,1:T(8,128)(2,1)S(1)} %bitcast_multiply_fusion.1), channel_id=1, source_target_pairs={{0,24},{8,0},{16,8},{24,16},{1,25},{9,1},{17,9},{25,17},{2,26},{10... | collective-permute-start | bytes 1769480 | tf_op jit(solution)/shard_map/ppermute | solution.py:10
  22.9 27.2 %collective-permute-start.1 = (bf16[768,384]{0,1:T(8,128)(2,1)S(1)}, bf16[768,384]{0,1:T(8,128)(2,1)S(1)}, u32[]{:S(2)}, u32[]{:S(2)}) collective-permute-start(bf16[768,384]{0,1:T(8,128)(2,1)S(1)} %get-tuple-element.18), channel_id=1, source_target_pairs={{0,4},{1,5},{2,6},{3,7},{4,0},{5,1},{6,2},{7,3},{8,12},{9,13},{10,... | collective-permute-start | bytes 1769480 | tf_op jit(solution)/shard_map/ppermute | solution.py:10
  23.0 28.7 %collective-permute-start.4 = (bf16[768,384]{0,1:T(8,128)(2,1)S(1)}, bf16[768,384]{0,1:T(8,128)(2,1)S(1)}, u32[]{:S(2)}, u32[]{:S(2)}) collective-permute-start(bf16[768,384]{0,1:T(8,128)(2,1)S(1)} %get-tuple-element.19), channel_id=1, source_target_pairs={{0,16},{8,24},{16,0},{24,8},{1,17},{9,25},{17,1},{25,9},{2,18},{10... | collective-permute-start | bytes 1769480 | tf_op jit(solution)/shard_map/ppermute | solution.py:10
  50.2 15.3 %collective-permute-start.5 = (bf16[768,384]{0,1:T(8,128)(2,1)S(1)}, bf16[768,384]{0,1:T(8,128)(2,1)S(1)}, u32[]{:S(2)}, u32[]{:S(2)}) collective-permute-start(bf16[768,384]{0,1:T(8,128)(2,1)S(1)} %broadcast_select_fusion.9), channel_id=1, source_target_pairs={{0,6},{1,7},{2,0},{3,1},{4,2},{5,3},{6,4},{7,5},{8,14},{9,15},{10,... | collective-permute-start | bytes 1769480 | tf_op jit(solution)/shard_map/ppermute | solution.py:10
  51.8 17.0 %collective-permute-start.7 = (bf16[768,384]{0,1:T(8,128)(2,1)S(1)}, bf16[768,384]{0,1:T(8,128)(2,1)}, u32[]{:S(2)}, u32[]{:S(2)}) collective-permute-start(bf16[768,384]{0,1:T(8,128)(2,1)S(1)} %broadcast_select_fusion.5), channel_id=1, source_target_pairs={{0,24},{8,0},{16,8},{24,16},{1,25},{9,1},{17,9},{25,17},{2,26},{10... | collective-permute-start | bytes 1769480 | tf_op jit(solution)/shard_map/ppermute | solution.py:10
  65.5 15.1 %collective-permute-start.8 = (bf16[768,384]{0,1:T(8,128)(2,1)S(1)}, bf16[768,384]{0,1:T(8,128)(2,1)}, u32[]{:S(2)}, u32[]{:S(2)}) collective-permute-start(bf16[768,384]{0,1:T(8,128)(2,1)S(1)} %collective-permute-done.5), channel_id=1, source_target_pairs={{0,6},{1,7},{2,0},{3,1},{4,2},{5,3},{6,4},{7,5},{8,14},{9,15},{10,... | collective-permute-start | bytes 1769480 | tf_op jit(solution)/shard_map/ppermute | solution.py:10
  68.8 16.6 %collective-permute-start.10 = (bf16[768,384]{0,1:T(8,128)(2,1)}, bf16[768,384]{0,1:T(8,128)(2,1)}, u32[]{:S(2)}, u32[]{:S(2)}) collective-permute-start(bf16[768,384]{0,1:T(8,128)(2,1)} %collective-permute-done.7), channel_id=1, source_target_pairs={{0,24},{8,0},{16,8},{24,16},{1,25},{9,1},{17,9},{25,17},{2,26},{10... | collective-permute-start | bytes 1769480 | tf_op jit(solution)/shard_map/ppermute | solution.py:10
  72.1 16.6 %collective-permute-start.6 = (bf16[768,384]{0,1:T(8,128)(2,1)S(1)}, bf16[768,384]{0,1:T(8,128)(2,1)}, u32[]{:S(2)}, u32[]{:S(2)}) collective-permute-start(bf16[768,384]{0,1:T(8,128)(2,1)S(1)} %collective-permute-done.5), channel_id=1, source_target_pairs={{0,1},{1,0},{2,3},{3,2},{4,5},{5,4},{6,7},{7,6},{8,9},{9,8},{10,11... | collective-permute-start | bytes 1769480 | tf_op jit(solution)/shard_map/ppermute | solution.py:20
  72.1 24.3 %collective-permute-start.2 = (bf16[768,384]{0,1:T(8,128)(2,1)S(1)}, bf16[768,384]{0,1:T(8,128)(2,1)}, u32[]{:S(2)}, u32[]{:S(2)}) collective-permute-start(bf16[768,384]{0,1:T(8,128)(2,1)S(1)} %broadcast_select_fusion.9), channel_id=1, source_target_pairs={{0,1},{1,0},{2,3},{3,2},{4,5},{5,4},{6,7},{7,6},{8,9},{9,8},{10,11... | collective-permute-start | bytes 1769480 | tf_op jit(solution)/shard_map/ppermute | solution.py:20
  80.7 15.7 %collective-permute-start.11 = (bf16[768,384]{0,1:T(8,128)(2,1)}, bf16[768,384]{0,1:T(8,128)(2,1)}, u32[]{:S(2)}, u32[]{:S(2)}) collective-permute-start(bf16[768,384]{0,1:T(8,128)(2,1)} %collective-permute-done.8), channel_id=1, source_target_pairs={{0,6},{1,7},{2,0},{3,1},{4,2},{5,3},{6,4},{7,5},{8,14},{9,15},{10,... | collective-permute-start | bytes 1769480 | tf_op jit(solution)/shard_map/ppermute | solution.py:10
  85.3 13.0 %collective-permute-start.9 = (bf16[768,384]{0,1:T(8,128)(2,1)}, bf16[768,384]{0,1:T(8,128)(2,1)S(1)}, u32[]{:S(2)}, u32[]{:S(2)}) collective-permute-start(bf16[768,384]{0,1:T(8,128)(2,1)} %collective-permute-done.8), channel_id=1, source_target_pairs={{0,1},{1,0},{2,3},{3,2},{4,5},{5,4},{6,7},{7,6},{8,9},{9,8},{10,11... | collective-permute-start | bytes 1769480 | tf_op jit(solution)/shard_map/ppermute | solution.py:20
  85.3 16.9 %collective-permute-start.13 = (bf16[768,384]{0,1:T(8,128)(2,1)}, bf16[768,384]{0,1:T(8,128)(2,1)S(1)}, u32[]{:S(2)}, u32[]{:S(2)}) collective-permute-start(bf16[768,384]{0,1:T(8,128)(2,1)} %collective-permute-done.10), channel_id=1, source_target_pairs={{0,24},{8,0},{16,8},{24,16},{1,25},{9,1},{17,9},{25,17},{2,26},{10... | collective-permute-start | bytes 1769480 | tf_op jit(solution)/shard_map/ppermute | solution.py:10
  96.4 5.9 %collective-permute-start.12 = (bf16[768,384]{0,1:T(8,128)(2,1)}, bf16[768,384]{0,1:T(8,128)(2,1)S(1)}, u32[]{:S(2)}, u32[]{:S(2)}) collective-permute-start(bf16[768,384]{0,1:T(8,128)(2,1)} %collective-permute-done.11), channel_id=1, source_target_pairs={{0,1},{1,0},{2,3},{3,2},{4,5},{5,4},{6,7},{7,6},{8,9},{9,8},{10,11... | collective-permute-start | bytes 1769480 | tf_op jit(solution)/shard_map/ppermute | solution.py:20
  104.6 16.5 %collective-permute-start.14 = (bf16[768,384]{0,1:T(8,128)(2,1)S(1)}, bf16[768,384]{0,1:T(8,128)(2,1)S(1)}, u32[]{:S(2)}, u32[]{:S(2)}) collective-permute-start(bf16[768,384]{0,1:T(8,128)(2,1)S(1)} %fusion.3), channel_id=1, source_target_pairs={{0,8},{8,16},{16,24},{24,0},{1,9},{9,17},{17,25},{25,1},{2,10},{10... | collective-permute-start | bytes 1769480 | tf_op jit(solution)/shard_map/ppermute | solution.py:10
  121.2 16.9 %collective-permute-start.15 = (bf16[768,384]{0,1:T(8,128)(2,1)S(1)}, bf16[768,384]{0,1:T(8,128)(2,1)S(1)}, u32[]{:S(2)}, u32[]{:S(2)}) collective-permute-start(bf16[768,384]{0,1:T(8,128)(2,1)S(1)} %broadcast_select_fusion.10), channel_id=1, source_target_pairs={{0,2},{1,3},{2,4},{3,5},{4,6},{5,7},{6,0},{7,1},{8,10},{9,11},{10,... | collective-permute-start | bytes 1769480 | tf_op jit(solution)/shard_map/ppermute | solution.py:10
  138.2 14.2 %collective-permute-start.16 = (bf16[768,384]{0,1:T(8,128)(2,1)S(1)}, bf16[768,384]{0,1:T(8,128)(2,1)S(1)}, u32[]{:S(2)}, u32[]{:S(2)}) collective-permute-start(bf16[768,384]{0,1:T(8,128)(2,1)S(1)} %broadcast_select_fusion), channel_id=1, source_target_pairs={{0,16},{8,24},{16,0},{24,8},{1,17},{9,25},{17,1},{25,9},{2,18},{10... | collective-permute-start | bytes 1769480 | tf_op jit(solution)/shard_map/ppermute | solution.py:10
  152.5 26.3 %collective-permute-start.17 = (bf16[768,384]{0,1:T(8,128)(2,1)S(1)}, bf16[768,384]{0,1:T(8,128)(2,1)S(1)}, u32[]{:S(2)}, u32[]{:S(2)}) collective-permute-start(bf16[768,384]{0,1:T(8,128)(2,1)S(1)} %broadcast_select_fusion.11), channel_id=1, source_target_pairs={{0,4},{1,5},{2,6},{3,7},{4,0},{5,1},{6,2},{7,3},{8,12},{9,13},{10,... | collective-permute-start | bytes 1769480 | tf_op jit(solution)/shard_map/ppermute | solution.py:10
  184.1 15.4 %collective-permute-start.19 = (bf16[768,384]{0,1:T(8,128)(2,1)S(1)}, bf16[768,384]{0,1:T(8,128)(2,1)S(1)}, u32[]{:S(2)}, u32[]{:S(2)}) collective-permute-start(bf16[768,384]{0,1:T(8,128)(2,1)S(1)} %bitcast_multiply_fusion), channel_id=1, source_target_pairs={{0,6},{1,7},{2,0},{3,1},{4,2},{5,3},{6,4},{7,5},{8,14},{9,15},{10,... | collective-permute-start | bytes 1769480 | tf_op jit(solution)/shard_map/ppermute | solution.py:10
  185.9 15.1 %collective-permute-start.22 = (bf16[768,384]{0,1:T(8,128)(2,1)S(1)}, bf16[768,384]{0,1:T(8,128)(2,1)S(1)}, u32[]{:S(2)}, u32[]{:S(2)}) collective-permute-start(bf16[768,384]{0,1:T(8,128)(2,1)S(1)} %bitcast_multiply_fusion), channel_id=1, source_target_pairs={{0,24},{8,0},{16,8},{24,16},{1,25},{9,1},{17,9},{25,17},{2,26},{10... | collective-permute-start | bytes 1769480 | tf_op jit(solution)/shard_map/ppermute | solution.py:10
  201.1 27.6 %collective-permute-start.20 = (bf16[768,384]{0,1:T(8,128)(2,1)S(1)}, bf16[768,384]{0,1:T(8,128)(2,1)S(1)}, u32[]{:S(2)}, u32[]{:S(2)}) collective-permute-start(bf16[768,384]{0,1:T(8,128)(2,1)S(1)} %get-tuple-element.16), channel_id=1, source_target_pairs={{0,4},{1,5},{2,6},{3,7},{4,0},{5,1},{6,2},{7,3},{8,12},{9,13},{10,... | collective-permute-start | bytes 1769480 | tf_op jit(solution)/shard_map/ppermute | solution.py:10
  201.2 29.1 %collective-permute-start.23 = (bf16[768,384]{0,1:T(8,128)(2,1)S(1)}, bf16[768,384]{0,1:T(8,128)(2,1)S(1)}, u32[]{:S(2)}, u32[]{:S(2)}) collective-permute-start(bf16[768,384]{0,1:T(8,128)(2,1)S(1)} %get-tuple-element.17), channel_id=1, source_target_pairs={{0,16},{8,24},{16,0},{24,8},{1,17},{9,25},{17,1},{25,9},{2,18},{10... | collective-permute-start | bytes 1769480 | tf_op jit(solution)/shard_map/ppermute | solution.py:10
  228.8 15.4 %collective-permute-start.24 = (bf16[768,384]{0,1:T(8,128)(2,1)S(1)}, bf16[768,384]{0,1:T(8,128)(2,1)}, u32[]{:S(2)}, u32[]{:S(2)}) collective-permute-start(bf16[768,384]{0,1:T(8,128)(2,1)S(1)} %broadcast_select_fusion.8), channel_id=1, source_target_pairs={{0,6},{1,7},{2,0},{3,1},{4,2},{5,3},{6,4},{7,5},{8,14},{9,15},{10,... | collective-permute-start | bytes 1769480 | tf_op jit(solution)/shard_map/ppermute | solution.py:10
  230.3 17.1 %collective-permute-start.26 = (bf16[768,384]{0,1:T(8,128)(2,1)S(1)}, bf16[768,384]{0,1:T(8,128)(2,1)}, u32[]{:S(2)}, u32[]{:S(2)}) collective-permute-start(bf16[768,384]{0,1:T(8,128)(2,1)S(1)} %broadcast_select_fusion.4), channel_id=1, source_target_pairs={{0,24},{8,0},{16,8},{24,16},{1,25},{9,1},{17,9},{25,17},{2,26},{10... | collective-permute-start | bytes 1769480 | tf_op jit(solution)/shard_map/ppermute | solution.py:10
  244.2 15.5 %collective-permute-start.27 = (bf16[768,384]{0,1:T(8,128)(2,1)}, bf16[768,384]{0,1:T(8,128)(2,1)S(1)}, u32[]{:S(2)}, u32[]{:S(2)}) collective-permute-start(bf16[768,384]{0,1:T(8,128)(2,1)} %collective-permute-done.24), channel_id=1, source_target_pairs={{0,6},{1,7},{2,0},{3,1},{4,2},{5,3},{6,4},{7,5},{8,14},{9,15},{10,... | collective-permute-start | bytes 1769480 | tf_op jit(solution)/shard_map/ppermute | solution.py:10
  247.4 17.2 %collective-permute-start.29 = (bf16[768,384]{0,1:T(8,128)(2,1)}, bf16[768,384]{0,1:T(8,128)(2,1)}, u32[]{:S(2)}, u32[]{:S(2)}) collective-permute-start(bf16[768,384]{0,1:T(8,128)(2,1)} %collective-permute-done.26), channel_id=1, source_target_pairs={{0,24},{8,0},{16,8},{24,16},{1,25},{9,1},{17,9},{25,17},{2,26},{10... | collective-permute-start | bytes 1769480 | tf_op jit(solution)/shard_map/ppermute | solution.py:10
  249.4 17.2 %collective-permute-start.25 = (bf16[768,384]{0,1:T(8,128)(2,1)}, bf16[768,384]{0,1:T(8,128)(2,1)}, u32[]{:S(2)}, u32[]{:S(2)}) collective-permute-start(bf16[768,384]{0,1:T(8,128)(2,1)} %collective-permute-done.24), channel_id=1, source_target_pairs={{0,1},{1,0},{2,3},{3,2},{4,5},{5,4},{6,7},{7,6},{8,9},{9,8},{10,11... | collective-permute-start | bytes 1769480 | tf_op jit(solution)/shard_map/ppermute | solution.py:20
  259.6 15.2 %collective-permute-start.30 = (bf16[768,384]{0,1:T(8,128)(2,1)S(1)}, bf16[768,384]{0,1:T(8,128)(2,1)S(1)}, u32[]{:S(2)}, u32[]{:S(2)}) collective-permute-start(bf16[768,384]{0,1:T(8,128)(2,1)S(1)} %collective-permute-done.27), channel_id=1, source_target_pairs={{0,6},{1,7},{2,0},{3,1},{4,2},{5,3},{6,4},{7,5},{8,14},{9,15},{10,... | collective-permute-start | bytes 1769480 | tf_op jit(solution)/shard_map/ppermute | solution.py:10
  263.8 11.0 %collective-permute-start.21 = (bf16[768,384]{0,1:T(8,128)(2,1)S(1)}, bf16[768,384]{0,1:T(8,128)(2,1)}, u32[]{:S(2)}, u32[]{:S(2)}) collective-permute-start(bf16[768,384]{0,1:T(8,128)(2,1)S(1)} %broadcast_select_fusion.8), channel_id=1, source_target_pairs={{0,1},{1,0},{2,3},{3,2},{4,5},{5,4},{6,7},{7,6},{8,9},{9,8},{10,11... | collective-permute-start | bytes 1769480 | tf_op jit(solution)/shard_map/ppermute | solution.py:20
  264.0 12.7 %collective-permute-start.28 = (bf16[768,384]{0,1:T(8,128)(2,1)S(1)}, bf16[768,384]{0,1:T(8,128)(2,1)S(1)}, u32[]{:S(2)}, u32[]{:S(2)}) collective-permute-start(bf16[768,384]{0,1:T(8,128)(2,1)S(1)} %collective-permute-done.27), channel_id=1, source_target_pairs={{0,1},{1,0},{2,3},{3,2},{4,5},{5,4},{6,7},{7,6},{8,9},{9,8},{10,11... | collective-permute-start | bytes 1769480 | tf_op jit(solution)/shard_map/ppermute | solution.py:20
  264.6 15.7 %collective-permute-start.32 = (bf16[768,384]{0,1:T(8,128)(2,1)}, bf16[768,384]{0,1:T(8,128)(2,1)S(1)}, u32[]{:S(2)}, u32[]{:S(2)}) collective-permute-start(bf16[768,384]{0,1:T(8,128)(2,1)} %collective-permute-done.29), channel_id=1, source_target_pairs={{0,24},{8,0},{16,8},{24,16},{1,25},{9,1},{17,9},{25,17},{2,26},{10... | collective-permute-start | bytes 1769480 | tf_op jit(solution)/shard_map/ppermute | solution.py:10
  274.8 5.5 %collective-permute-start.31 = (bf16[768,384]{0,1:T(8,128)(2,1)S(1)}, bf16[768,384]{0,1:T(8,128)(2,1)S(1)}, u32[]{:S(2)}, u32[]{:S(2)}) collective-permute-start(bf16[768,384]{0,1:T(8,128)(2,1)S(1)} %collective-permute-done.30), channel_id=1, source_target_pairs={{0,1},{1,0},{2,3},{3,2},{4,5},{5,4},{6,7},{7,6},{8,9},{9,8},{10,11... | collective-permute-start | bytes 1769480 | tf_op jit(solution)/shard_map/ppermute | solution.py:20
  (4 other events, 46.9 us)
where the time goes:
time: 325 us; the launch traced here: 324 us
  waiting for transfers between devices  203 us (62%)
  starting transfers between devices  50.9 us (16%)
  blocking collectives  38.6 us (12%)
  matrix products  16.2 us (5%)
  local copies, waits for them, and re-layouts  7.83 us (2%)
  other arithmetic  5.83 us (2%)
    ppermute x24, waiting for transfers between devices, passed_along(): return lax.ppermute(value, axis, pairs)  202 us
    ppermute x24, starting transfers between devices, passed_along(): return lax.ppermute(value, axis, pairs)  49.7 us
    psum x1, blocking collectives, body(): totals = lax.psum((trace_one, trace_two), ('row', 'col'))  38.6 us
    dot_general x8, matrix products, multiply(): accum = accum + jnp.dot(panel, right, preferred_element_type=jnp.float32)  16.2 us
  transfers between devices with their start and end apart: 33, of which 19 were waited for; matrix products, arithmetic and copies ran while one was open for 5% of the time, Pallas kernels for 0%

commit v1 on v0

v1 whole, which is shorter than its diff:
```python
import jax
import jax.numpy as jnp
from jax import lax
from jax.sharding import PartitionSpec as P


def expand(mask, bdim, dtype):
    return jnp.repeat(jnp.repeat(mask, bdim, axis=0), bdim, axis=1).astype(dtype)


def product(left, right):
    steps, _, inner = left.shape
    right = right.reshape(steps, inner, right.shape[1])
    total = jnp.dot(left[0], right[0], preferred_element_type=jnp.float32)
    for step in range(1, steps):
        total = total + jnp.dot(left[step], right[step], preferred_element_type=jnp.float32)
    return total


def body(density, pattern, kept_slots, owner_shift, owner_slot):
    rows, cols = density.shape
    nrb, ncb = pattern.shape[1:]
    bdim = rows // nrb
    nrow, ncol = lax.axis_size("row"), lax.axis_size("col")
    nblocks = nrow * nrb
    row_index, col_index = lax.axis_index("row"), lax.axis_index("col")

    blocks = jnp.arange(nblocks, dtype=jnp.int32)
    local = blocks % nrb
    target_group = (blocks // nrb + owner_shift[local]) % nrow
    target = target_group * nrb + owner_slot[target_group, local]
    source = jnp.argsort(target).astype(jnp.int32)
    row_blocks = row_index * nrb + jnp.arange(nrb, dtype=jnp.int32)
    col_blocks = col_index * ncb + jnp.arange(ncb, dtype=jnp.int32)
    source_rows = source[row_blocks]
    source_cols = source[col_blocks]
    pattern_row = lax.all_gather(pattern[1], "col", axis=1, tiled=True)
    pattern_col = lax.all_gather(pattern[1], "row", axis=0, tiled=True)

    slots = jnp.arange(nrb * ncb, dtype=jnp.int32)
    keep = jnp.any(kept_slots[:, 0, 0, :, None] == slots, axis=1).reshape(2, nrb, ncb)

    operand = density * expand(pattern[0], bdim, density.dtype)
    left = lax.all_gather(operand, "col")
    right = lax.all_gather(operand, "row", axis=0, tiled=True)
    first = (product(left, right) * expand(keep[0], bdim, jnp.float32)).astype(jnp.bfloat16)

    by_row = lax.all_gather(first, "row", axis=0, tiled=True).reshape(nblocks, bdim, cols)
    by_col = lax.all_gather(first, "col")
    picked_rows = jnp.take(by_row, source_rows, axis=0).reshape(rows, cols)
    picked_rows = picked_rows * expand(pattern_row[:, target[col_blocks]], bdim, first.dtype)

    def pick(panels):
        return jnp.concatenate(
            [
                lax.dynamic_slice(
                    panels,
                    (source_cols[j] // ncb, 0, source_cols[j] % ncb * bdim),
                    (1, rows, bdim),
                )[0]
                for j in range(ncb)
            ],
            axis=1,
        )

    picked_cols = pick(by_col) * expand(pattern_col[target[row_blocks]], bdim, first.dtype)
    left = lax.all_gather(picked_rows, "col")
    right = lax.all_gather(picked_cols, "row", axis=0, tiled=True)
    square = product(left, right)
    update = 2.0 * pick(left).astype(jnp.float32) - square
    second = (update * expand(keep[1], bdim, jnp.float32)).astype(jnp.bfloat16)

    global_row = row_index * rows + jnp.arange(rows, dtype=jnp.int32)[:, None]
    global_col = col_index * cols + jnp.arange(cols, dtype=jnp.int32)[None, :]
    on_diagonal = global_row == global_col
    traces = jnp.stack(
        [jnp.sum(jnp.where(on_diagonal, t.astype(jnp.float32), 0.0)) for t in (first, second)]
    )
    return second, lax.psum(traces, ("row", "col"))


def solution(mesh):
    placed = (P("row", "col"), P(None, "row", "col"), P(None, "row", "col", None), P(), P())
    return jax.shard_map(
        body, mesh=mesh, in_specs=placed, out_specs=(P("row", "col"), P()), check_vma=False
    )
```

time: 325 us -> 352 us (1.083)
  starting transfers between devices: 50.9 us -> 0.24 us
  waiting for transfers between devices: 203 us -> 231 us
  blocking collectives: 38.6 us -> 60.2 us
  between operations: 0.99 us -> 20.2 us
  local copies, waits for them, and re-layouts: 7.83 us -> 15.3 us
    all_gather x0 -> x6, waiting for transfers between devices: none -> 229 us  [the longest x1 53.9 us: body(): left = lax.all_gather(operand, 'col')]
    ppermute x33 -> x0, waiting for transfers between devices: 203 us -> none  [the longest x24 202 us: passed_along(): return lax.ppermute(value, axis, pairs)]
    ppermute x33 -> x0, starting transfers between devices: 50.9 us -> none  [the longest x24 49.7 us: passed_along(): return lax.ppermute(value, axis, pairs)]
    all_gather x0 -> x2, blocking collectives: none -> 20.9 us  [the longest x1 12.7 us: body(): pattern_row = lax.all_gather(pattern[1], 'col', axis=1, tiled=True)]
    gather x7 -> x10, local copies, waits for them, and re-layouts: 3.96 us -> 7.65 us  [the longest x1 2.34 us: body(): picked_rows = jnp.take(by_row, source_rows, axis=0).reshape(rows, cols)]
    dot_general x8 -> x16, matrix products: 16.2 us -> 18.4 us  [the longest x14 14.7 us: product(): jnp.dot(left[step], right[step], preferred_element_type=jnp.float32)]
  transfers between devices with their start and end apart: 33 -> 6, of which waited for: 19 -> 6; matrix products, arithmetic and copies ran while one was open for 5% -> 5% of each run, Pallas kernels for 0% -> 0%
where the time goes in v1:
time: 352 us
  waiting for transfers between devices  231 us (66%)
  blocking collectives  60.2 us (17%)
  between operations  20.2 us (6%)
  matrix products  18.4 us (5%)
  local copies, waits for them, and re-layouts  15.3 us (4%)
  other arithmetic  6.82 us (2%)
    all_gather x1, waiting for transfers between devices, body(): left = lax.all_gather(operand, 'col')  53.9 us
    all_gather x1, waiting for transfers between devices, body(): left = lax.all_gather(picked_rows, 'col')  48.7 us
    psum x1, blocking collectives, body(): return (second, lax.psum(traces, ('row', 'col')))  39.3 us
    all_gather x1, waiting for transfers between devices, body(): right = lax.all_gather(operand, 'row', axis=0, tiled=True)  38.7 us
    all_gather x1, waiting for transfers between devices, body(): right = lax.all_gather(picked_cols, 'row', axis=0, tiled=True)  36.9 us
    all_gather x1, waiting for transfers between devices, body(): by_col = lax.all_gather(first, 'col')  33.7 us
    all_gather x1, waiting for transfers between devices, body(): lax.all_gather(first, 'row', axis=0, tiled=True)  17.5 us
    dot_general x14, matrix products, product(): jnp.dot(left[step], right[step], preferred_element_type=jnp.float32)  14.7 us
  transfers between devices with their start and end apart: 6, of which 6 were waited for; matrix products, arithmetic and copies ran while one was open for 5% of the time, Pallas kernels for 0%

profile of v1, /device:TPU:0, one launch (start us, length us, event | category | flops | bytes accessed | tf_op | source)
XLA Modules:
  0.0 351.8 jit_solution(8919520004415747361)
XLA Ops:
  7.2 0.8 slice_convert_fusion
  8.1 1.3 copy.66
  9.4 0.9 bitcast_multiply_fusion
  10.3 0.7 all-gather.19.cloned.1.call-update
  12.0 38.7 %all-gather.11.cloned.1.call-done = bf16[3072,384]{0,1:T(8,128)(2,1)} async-done(((bf16[768,384]{0,1:T(8,128)(2,1)}), bf16[3072,384]{0,1:T(8,128)(2,1)}) %all-gather.11.cloned.1.call-update) | async-done | bytes 2359312 | tf_op jit(solution)/shard_map/all_gather | solution.py:45
  50.7 53.9 %all-gather.19.cloned.1.call-done = bf16[6144,384]{0,1:T(8,128)(2,1)} async-done(((bf16[768,384]{0,1:T(8,128)(2,1)}), bf16[6144,384]{0,1:T(8,128)(2,1)}) %all-gather.19.cloned.1.call-update) | async-done | bytes 4718608 | tf_op jit(solution)/shard_map/all_gather | solution.py:44
  104.5 1.8 fusion.15
  106.4 1.7 convolution_add_fusion.13
  108.1 1.7 convolution_add_fusion.12
  112.1 1.4 fusion.3
  114.2 0.7 gather_fusion
  115.0 0.8 gather_fusion.1
  115.9 1.6 sort.17
  118.1 12.7 %all-gather.1 = s32[1,6,24]{1,0,2:T(1,128)S(1)} all-gather(s32[1,6,3]{1,0,2:T(1,128)S(1)} %get-tuple-element.15), channel_id=3, replica_groups=mesh['row'=4,'col'=8] {'col'}, dimensions={2}, use_global_device_ids=true | all-gather | bytes 648 | tf_op jit(solution)/shard_map/all_gather | solution.py:37
  131.8 0.6 gather_fusion.2
  132.6 17.5 %all-gather.13.cloned.1.call-done = bf16[3072,384]{1,0:T(8,128)(2,1)} async-done(((bf16[768,384]{1,0:T(8,128)(2,1)}), bf16[3072,384]{1,0:T(8,128)(2,1)}) %all-gather.13.cloned.1.call-update) | async-done | bytes 2359312 | tf_op jit(solution)/shard_map/all_gather | solution.py:48
  150.1 2.3 gather_fusion.3
  152.5 1.0 fusion.17
  160.5 0.6 gather_fusion.7
  161.2 8.3 %all-gather.3 = s32[1,24,3]{2,0,1:T(1,128)S(1)} all-gather(s32[1,6,3]{2,0,1:T(1,128)S(1)} %copy.72), channel_id=5, replica_groups=mesh['row'=4,'col'=8] {'row'}, dimensions={1}, use_global_device_ids=true | all-gather | bytes 360 | tf_op jit(solution)/shard_map/all_gather | solution.py:38
  170.2 33.7 %all-gather.21.cloned.1.call-done = bf16[6144,384]{1,0:T(8,128)(2,1)} async-done(((bf16[768,384]{1,0:T(8,128)(2,1)}), bf16[6144,384]{1,0:T(8,128)(2,1)}) %all-gather.21.cloned.1.call-update) | async-done | bytes 4718608 | tf_op jit(solution)/shard_map/all_gather | solution.py:49
  203.9 1.2 constant_dynamic-slice_fusion.2
  205.5 0.9 maximum_multiply_fusion
  207.3 48.7 %all-gather.15.cloned.1.call-done = bf16[8,768,384]{2,1,0:T(8,128)(2,1)} async-done(((bf16[1,768,384]{2,1,0:T(8,128)(2,1)}), bf16[8,768,384]{2,1,0:T(8,128)(2,1)}) %all-gather.15.cloned.1.call-update) | async-done | bytes 4718608 | tf_op jit(solution)/shard_map/all_gather | solution.py:67
  256.0 1.2 dynamic-slice_bitcast_fusion.2
  257.2 36.9 %all-gather.17.cloned.1.call-done = bf16[3072,384]{0,1:T(8,128)(2,1)} async-done(((bf16[768,384]{0,1:T(8,128)(2,1)}), bf16[3072,384]{0,1:T(8,128)(2,1)}) %all-gather.17.cloned.1.call-update) | async-done | bytes 2359312 | tf_op jit(solution)/shard_map/all_gather | solution.py:68
  294.0 1.8 fusion.7
  295.9 1.7 convolution_add_fusion.6
  297.6 1.6 convolution_add_fusion.5
  302.0 2.2 fusion.5
  304.2 1.4 pad_maximum_fusion
  305.7 39.3 %psum.7 = f32[2]{0:T(128)} all-reduce(f32[2]{0:T(128)S(1)} %pad_maximum_fusion), channel_id=1, replica_groups=mesh['row'=4,'col'=8] {'row','col'}, use_global_device_ids=true, to_apply=%region_4.5 | all-reduce | flops 2 | bytes 16 | tf_op jit(solution)/shard_map/psum | solution.py:79
  (89 shorter events, 12.0 us)
Async XLA Ops:
  7.2 107.8 %copy-start = (s32[4,6]{1,0:T(4,128)S(1)}, s32[4,6]{1,0:T(4,128)}, u32[]{:S(2)}) copy-start(s32[4,6]{1,0:T(4,128)} %param.9) | copy-start | bytes 292
  7.2 43.5 %all-gather.11.cloned.1.call-start = ((), (), s32[]{:S(2)}) async-start(), calls=%async_computation | async-start | bytes 2949120 | tf_op jit(solution)/shard_map/all_gather | solution.py:45
  9.4 1.7 copy-start.7
  10.3 94.3 %all-gather.19.cloned.1.call-start = ((), (), s32[]{:S(2)}) async-start(), calls=%async_computation.4 | async-start | bytes 5308416 | tf_op jit(solution)/shard_map/all_gather | solution.py:44
  11.0 139.1 %all-gather.13.cloned.1.call-start = ((), (), s32[]{:S(2)}) async-start(), calls=%async_computation.1 | async-start | bytes 2949120 | tf_op jit(solution)/shard_map/all_gather | solution.py:48
  104.5 3.6 %copy-start.4 = (bf16[6144,384]{0,1:T(8,128)(2,1)S(1)}, bf16[6144,384]{0,1:T(8,128)(2,1)}, u32[]{:S(2)}) copy-start(bf16[6144,384]{0,1:T(8,128)(2,1)} %all-gather.19.cloned.1.call-done) | copy-start | bytes 14155780
  108.1 1.8 copy-start.5
  113.5 0.7 copy-start.1
  113.6 90.3 %all-gather.21.cloned.1.call-start = ((), (), s32[]{:S(2)}) async-start(), calls=%async_computation.5 | async-start | bytes 5308416 | tf_op jit(solution)/shard_map/all_gather | solution.py:49
  114.1 141.9 %all-gather.15.cloned.1.call-start = ((), (), s32[]{:S(2)}) async-start(), calls=%async_computation.2 | async-start | bytes 5308416 | tf_op jit(solution)/shard_map/all_gather | solution.py:67
  153.5 140.6 %all-gather.17.cloned.1.call-start = ((), (), s32[]{:S(2)}) async-start(), calls=%async_computation.3 | async-start | bytes 2949120 | tf_op jit(solution)/shard_map/all_gather | solution.py:68
  294.0 3.5 copy-start.3
  297.6 1.8 copy-start.6
  300.9 1.1 copy-start.2
Sparse Core Ops, SparseCore 0:
  10.4 40.1 all-gather.10
  52.8 51.6 all-gather.18
  113.7 36.3 all-gather.12
  152.2 51.6 all-gather.20
  205.4 50.5 all-gather.14
  257.7 36.2 all-gather.16

commit v2 on v1

v2 whole, which is shorter than its diff:
```python
import functools

import jax
import jax.numpy as jnp
from jax import lax
from jax.experimental import pallas as pl
from jax.experimental.pallas import tpu as pltpu
from jax.sharding import PartitionSpec as P

MESH = pl.DeviceIdType.MESH
F32 = jnp.float32
BF16 = jnp.bfloat16


def kernel(
    nrow, ncol, nrb, ncb, at,
    meta, dens, pat, out, traces,
    panel_0, panel_1, panel_2, column_0, column_1, column_2, pat_row, pat_col, sum_row, sum_col, acc, diag,
    p_recv, p_up, p_down, p_part, c_recv, c_send,
    pr_recv, pr_send, pc_recv, pc_send, sr_recv, sr_send, sc_recv, sc_send,
):
    panel, column = (panel_0, panel_1, panel_2), (column_0, column_1, column_2)
    rows, cols = dens.shape
    bdim = rows // nrb
    groups = ncol // 2
    r, c = lax.axis_index("row"), lax.axis_index("col")
    g, parity = c // 2, c % 2
    partner = 2 * g + 1 - parity

    def other_row(d):
        return lax.rem(r + d, nrow)

    def other_col(d):
        return lax.rem(c + d, ncol)

    barrier = pltpu.get_barrier_semaphore()
    for d in range(1, nrow):
        pl.semaphore_signal(barrier, inc=1, device_id=(other_row(d), c), device_id_type=MESH)
    for d in range(1, ncol):
        pl.semaphore_signal(barrier, inc=1, device_id=(r, other_col(d)), device_id_type=MESH)
    pl.semaphore_wait(barrier, nrow + ncol - 2)

    def remote(ref, send, recv, device):
        return pltpu.make_async_remote_copy(
            src_ref=ref, dst_ref=ref, send_sem=send, recv_sem=recv,
            device_id=device, device_id_type=MESH,
        )

    def along_col(ph, slot, to, sem):
        return remote(panel[ph].at[slot], sem.at[ph, slot], p_recv.at[ph, slot], (r, to))

    def along_row(ph, slot, to, d):
        return remote(column[ph].at[slot], c_send.at[ph, d], c_recv.at[ph, slot], (to, c))

    def small_row(buf, send, recv, slot, d):
        return remote(buf.at[slot], send.at[d], recv.at[slot], (other_row(d), c))

    def small_col(buf, send, recv, slot, d):
        return remote(buf.at[slot], send.at[d], recv.at[slot], (r, other_col(d)))

    def begin(ph):
        @pl.when(g + 1 < groups)
        def _():
            along_col(ph, c, c + 2, p_up).start()

        @pl.when(g > 0)
        def _():
            along_col(ph, c, c - 2, p_down).start()

        along_col(ph, c, partner, p_part).start()
        for d in range(1, nrow):
            along_row(ph, r, other_row(d), d).start()

    def relay(ph, d):
        below, above = g - d, g + d

        @pl.when(below >= 0)
        def _():
            slot = 2 * below + parity
            along_col(ph, slot, partner, p_part).wait_recv()

            @pl.when(g + 1 < groups)
            def _():
                along_col(ph, slot, c + 2, p_up).start()

            along_col(ph, slot, partner, p_part).start()

        @pl.when(above < groups)
        def _():
            slot = 2 * above + parity
            along_col(ph, slot, partner, p_part).wait_recv()

            @pl.when(g > 0)
            def _():
                along_col(ph, slot, c - 2, p_down).start()

            along_col(ph, slot, partner, p_part).start()

    def from_partner(ph, group):
        along_col(ph, 2 * group + 1 - parity, partner, p_part).wait_recv()

    def columns_in(ph):
        for d in range(1, nrow):
            along_row(ph, other_row(d), other_row(1), d).wait_recv()

    def finish(ph):
        along_col(ph, c, partner, p_part).wait_send()

        @pl.when(g + 1 < groups)
        def _():
            along_col(ph, c, c + 2, p_up).wait_send()

        @pl.when(g > 0)
        def _():
            along_col(ph, c, c - 2, p_down).wait_send()

        for d in range(1, groups):
            below, above = g - d, g + d

            @pl.when(below >= 0)
            def _():
                slot = 2 * below + parity

                @pl.when(g + 1 < groups)
                def _():
                    along_col(ph, slot, c + 2, p_up).wait_send()

                along_col(ph, slot, partner, p_part).wait_send()

            @pl.when(above < groups)
            def _():
                slot = 2 * above + parity

                @pl.when(g > 0)
                def _():
                    along_col(ph, slot, c - 2, p_down).wait_send()

                along_col(ph, slot, partner, p_part).wait_send()

        for d in range(1, nrow):
            along_row(ph, r, other_row(d), d).wait_send()

    half = rows // 2

    def compute(ph, d):
        def side(s, _):
            group = g + (2 * s - 1) * d

            @pl.when((group >= 0) & (group < groups) & ((d > 0) | (s > 0)))
            def _():
                from_partner(ph, group)

                def part(q, _):
                    right = column[ph][group, pl.ds(q * ncb, ncb)].reshape(cols, cols)
                    for k in range(2):
                        here = pl.ds(k * half, half)
                        left = jnp.concatenate(
                            [panel[ph][2 * group + q, j, here, :] for j in range(ncb)], axis=1
                        )
                        acc[here, :] += jnp.dot(left, right, preferred_element_type=F32)
                    return 0

                lax.fori_loop(0, 2, part, 0)

            return 0

        lax.fori_loop(0, 2, side, 0)

    def multiply(ph):
        acc[...] = jnp.zeros_like(acc)
        first = min(2, groups - 1)
        for d in range(1, groups):
            relay(ph, d)
            if d == first:
                columns_in(ph)

                def early(e, _):
                    compute(ph, e)
                    return 0

                lax.fori_loop(0, first + 1, early, 0)
            elif d > first:
                compute(ph, d)

    def block(i, j):
        return pl.ds(i * bdim, bdim), pl.ds(j * bdim, bdim)

    def trace_of(ref_value):
        total = jnp.zeros((bdim, bdim), F32)
        eye = lax.broadcasted_iota(jnp.int32, (bdim, bdim), 0) == lax.broadcasted_iota(
            jnp.int32, (bdim, bdim), 1
        )
        for i in range(nrb):
            for j in range(ncb):
                hit = r * nrb + i == c * ncb + j
                total += jnp.where(eye & hit, ref_value(i, j), 0.0)
        return jnp.sum(total, axis=0, keepdims=True)

    for i in range(nrb):
        for j in range(ncb):
            value = dens[block(i, j)] * meta[at["occupied"] + i * ncb + j].astype(F32).astype(BF16)
            panel[0][c, j, pl.ds(i * bdim, bdim), :] = value
            column[0][r, i, :, pl.ds(j * bdim, bdim)] = value
    begin(0)
    pat_row[c] = pat[...]
    pat_col[r] = pat[...]
    for d in range(1, nrow):
        small_row(pat_col, pc_send, pc_recv, r, d).start()
    for d in range(1, ncol):
        small_col(pat_row, pr_send, pr_recv, c, d).start()

    multiply(0)
    for i in range(nrb):
        for j in range(ncb):
            keep = meta[at["keep"] + i * ncb + j].astype(F32)
            value = (acc[block(i, j)] * keep).astype(BF16)
            panel[1][c, j, pl.ds(i * bdim, bdim), :] = value
            column[1][r, i, :, pl.ds(j * bdim, bdim)] = value
    begin(1)
    diag[...] = jnp.zeros_like(diag)
    diag[0:1, :] = trace_of(lambda i, j: panel[1][c, j, pl.ds(i * bdim, bdim), :].astype(F32))

    for d in range(1, ncol):
        small_col(pat_row, pr_send, pr_recv, other_col(d), 1).wait_recv()
    for d in range(1, nrow):
        small_row(pat_col, pc_send, pc_recv, other_row(d), 1).wait_recv()
    for d in range(1, groups):
        relay(1, d)
    columns_in(1)
    for i in range(nrb):
        for j in range(ncb):
            mask = pat_row[
                meta[at["col_to_dev"] + j], meta[at["col_to_local"] + j] * nrb + i
            ].astype(BF16)
            value = column[1][meta[at["row_dev"] + i], meta[at["row_local"] + i], :, pl.ds(j * bdim, bdim)
            ]
            panel[2][c, j, pl.ds(i * bdim, bdim), :] = value * mask

    def others(k, _):
        @pl.when(k != g)
        def _():
            from_partner(1, k)

        return 0

    from_partner(1, g)
    lax.fori_loop(0, groups, others, 0)
    for j in range(ncb):
        for i in range(nrb):
            mask = pat_col[
                meta[at["row_to_dev"] + i], meta[at["row_to_local"] + i] + nrb * j
            ].astype(BF16)
            value = panel[1][meta[at["col_dev"] + j], meta[at["col_local"] + j], pl.ds(i * bdim, bdim), :
            ]
            column[2][r, i, :, pl.ds(j * bdim, bdim)] = value * mask
    begin(2)
    multiply(2)
    for j in range(ncb):
        for i in range(nrb):
            keep = meta[at["keep"] + (nrb + i) * ncb + j].astype(F32)
            operand = panel[2][meta[at["col_dev"] + j], meta[at["col_local"] + j], pl.ds(i * bdim, bdim), :
            ]
            out[block(i, j)] = ((2.0 * operand.astype(F32) - acc[block(i, j)]) * keep).astype(BF16)
    diag[1:2, :] = trace_of(lambda i, j: out[block(i, j)].astype(F32))

    sum_row[r] = diag[...]
    for d in range(1, nrow):
        small_row(sum_row, sr_send, sr_recv, r, d).start()
    for ph in range(3):
        finish(ph)
    for d in range(1, nrow):
        small_row(sum_row, sr_send, sr_recv, other_row(d), 1).wait_recv()
    sum_col[c] = functools.reduce(lambda a, b: a + b, [sum_row[k] for k in range(nrow)])
    for d in range(1, ncol):
        small_col(sum_col, sc_send, sc_recv, c, d).start()
    for d in range(1, ncol):
        small_col(sum_col, sc_send, sc_recv, other_col(d), 1).wait_recv()
    total = functools.reduce(lambda a, b: a + b, [sum_col[k] for k in range(ncol)])
    traces[...] = jnp.broadcast_to(jnp.sum(total, axis=1, keepdims=True), traces.shape)
    for d in range(1, nrow):
        small_row(pat_col, pc_send, pc_recv, r, d).wait_send()
        small_row(sum_row, sr_send, sr_recv, r, d).wait_send()
    for d in range(1, ncol):
        small_col(pat_row, pr_send, pr_recv, c, d).wait_send()
        small_col(sum_col, sc_send, sc_recv, c, d).wait_send()


def body(density, pattern, kept_slots, owner_shift, owner_slot):
    rows, cols = density.shape
    nrb, ncb = pattern.shape[1:]
    nrow, ncol = lax.axis_size("row"), lax.axis_size("col")
    nblocks = nrow * nrb
    row_index, col_index = lax.axis_index("row"), lax.axis_index("col")

    blocks = jnp.arange(nblocks, dtype=jnp.int32)
    shift = jnp.tile(owner_shift, nrow)
    group_to = (blocks // nrb + shift) % nrow
    local = jnp.tile(jnp.arange(nrb, dtype=jnp.int32), nrow)
    slot_hit = (group_to[:, None, None] == jnp.arange(nrow)[None, :, None]) & (
        local[:, None, None] == jnp.arange(nrb)[None, None, :]
    )
    target = group_to * nrb + jnp.sum(jnp.where(slot_hit, owner_slot[None], 0), axis=(1, 2))
    row_blocks = row_index * nrb + jnp.arange(nrb, dtype=jnp.int32)
    col_blocks = col_index * ncb + jnp.arange(ncb, dtype=jnp.int32)

    def source_of(wanted):
        return jnp.sum(jnp.where(wanted[:, None] == target[None, :], blocks[None, :], 0), axis=1)

    source_rows, source_cols = source_of(row_blocks), source_of(col_blocks)
    target_rows = lax.dynamic_slice(target, (row_index * nrb,), (nrb,))
    target_cols = lax.dynamic_slice(target, (col_index * ncb,), (ncb,))
    slots = jnp.arange(nrb * ncb, dtype=jnp.int32)
    keep = jnp.any(kept_slots[:, 0, 0, :, None] == slots, axis=1)
    fields = {
        "row_dev": source_rows // nrb,
        "row_local": source_rows % nrb,
        "col_dev": source_cols // ncb,
        "col_local": source_cols % ncb,
        "row_to_dev": target_rows // nrb,
        "row_to_local": target_rows % nrb,
        "col_to_dev": target_cols // ncb,
        "col_to_local": target_cols % ncb,
        "occupied": pattern[0].reshape(-1),
        "keep": keep.reshape(-1).astype(jnp.int32),
    }
    at, offset = {}, 0
    for name, value in fields.items():
        at[name] = offset
        offset += value.size
    meta = jnp.concatenate([value.astype(jnp.int32) for value in fields.values()])
    small = jnp.broadcast_to(pattern[1].T.astype(F32).reshape(ncb * nrb, 1, 1), (ncb * nrb, 1, 128))

    dma = pltpu.SemaphoreType.DMA
    vmem = pl.BlockSpec(memory_space=pltpu.VMEM)
    scratch = [
        *[pltpu.VMEM((ncol, ncb, rows, rows // nrb), BF16)] * 3,
        *[pltpu.VMEM((nrow, nrb, rows // nrb, cols), BF16)] * 3,
        pltpu.VMEM((ncol, ncb * nrb, 1, 128), F32),
        pltpu.VMEM((nrow, ncb * nrb, 1, 128), F32),
        pltpu.VMEM((nrow, 8, 128), F32),
        pltpu.VMEM((ncol, 8, 128), F32),
        pltpu.VMEM((rows, cols), F32),
        pltpu.VMEM((8, 128), F32),
    ]
    held = 3 * (nrow + ncol) * rows * cols * 2
    second, sums = pl.pallas_call(
        functools.partial(kernel, nrow, ncol, nrb, ncb, at),
        out_shape=(
            jax.ShapeDtypeStruct((rows, cols), BF16),
            jax.ShapeDtypeStruct((8, 128), F32),
        ),
        in_specs=[pl.BlockSpec(memory_space=pltpu.SMEM), vmem, vmem],
        out_specs=(vmem, vmem),
        scratch_shapes=scratch
        + [dma((3, ncol))] * 4
        + [dma((3, nrow))] * 2
        + [dma((ncol,))] * 2
        + [dma((nrow,))] * 4
        + [dma((ncol,))] * 2,
        compiler_params=pltpu.CompilerParams(
            collective_id=0, has_side_effects=True, vmem_limit_bytes=held + (10 << 20)
        ),
        cost_estimate=pl.CostEstimate(
            flops=4 * rows * cols * nblocks * rows // nrb,
            bytes_accessed=4 * rows * cols,
            transcendentals=0,
        ),
    )(meta, density, small)
    return second, sums[:2, 0]


def solution(mesh):
    placed = (P("row", "col"), P(None, "row", "col"), P(None, "row", "col", None), P(), P())
    return jax.shard_map(
        body, mesh=mesh, in_specs=placed, out_specs=(P("row", "col"), P()), check_vma=False
    )
```

time: 352 us -> 158 us (0.45)
  waiting for transfers between devices: 231 us -> 0 us
  Pallas kernels: 0 us -> 151 us
  blocking collectives: 60.2 us -> 0 us
  between operations: 20.2 us -> 0.72 us
  matrix products: 18.4 us -> 0 us
  local copies, waits for them, and re-layouts: 15.3 us -> 5.69 us
  other arithmetic: 6.82 us -> 0.81 us
    all_gather x6 -> x0, waiting for transfers between devices: 229 us -> none  [the longest x1 53.9 us: body(): left = lax.all_gather(operand, 'col')]
    pallas_call x0 -> x1, Pallas kernels: none -> 151 us  [body(): pl.pallas_call(functools.partial(kernel, nrow, ncol, nrb, ncb, at), out_s...]
    psum x1 -> x0, blocking collectives: 39.3 us -> none  [body(): return (second, lax.psum(traces, ('row', 'col')))]
    all_gather x2 -> x0, blocking collectives: 20.9 us -> none  [the longest x1 12.7 us: body(): pattern_row = lax.all_gather(pattern[1], 'col', axis=1, tiled=True)]
    dot_general x16 -> x0, matrix products: 18.4 us -> none  [the longest x14 14.7 us: product(): jnp.dot(left[step], right[step], preferred_element_type=jnp.float32)]
    gather x10 -> x0, local copies, waits for them, and re-layouts: 7.65 us -> none  [the longest x1 2.34 us: body(): picked_rows = jnp.take(by_row, source_rows, axis=0).reshape(rows, cols)]
  transfers between devices with their start and end apart: 6 -> 0, of which waited for: 6 -> 0; matrix products, arithmetic and copies ran while one was open for 5% -> 0% of each run, Pallas kernels for 0% -> 0%
where the time goes in v2:
time: 158 us
  Pallas kernels  151 us (96%)
  local copies, waits for them, and re-layouts  5.69 us (4%)
    pallas_call x1, Pallas kernels, body(): pl.pallas_call(functools.partial(kernel, nrow, ncol, nrb, ncb, at), out_s...  151 us
    unnamed x13, local copies, waits for them, and re-layouts  4.4 us

profile of v2, /device:TPU:0, one launch (start us, length us, event | category | flops | bytes accessed | tf_op | source)
XLA Modules:
  0.0 158.1 jit_solution(5427073178096197850)
XLA Ops:
  0.7 0.0 copy-start.4
  0.7 0.7 copy-done.4
  1.3 0.1 fusion
  1.4 0.0 copy-start.3
  1.4 0.1 reshape.133
  1.5 0.6 copy-done.3
  2.1 0.1 tile.7
  2.2 0.0 copy-start.1
  2.2 0.1 eq.91
  2.3 0.6 copy-done.1
  2.9 0.1 broadcast_in_dim.60
  3.0 0.1 copy.10
  3.1 0.0 copy-start.2
  3.1 0.1 reshape_squeeze.3
  3.2 0.6 copy-done.2
  3.8 0.1 copy.9
  3.9 0.1 select_reduce_fusion
  4.0 0.2 select_reduce_fusion.2
  4.2 0.2 select_reduce_fusion.1
  4.4 0.1 and_select_fusion.2
  4.4 0.1 and_select_fusion
  4.5 0.1 concatenate.3.meta
  4.6 0.1 broadcast_in_dim.61.pat
  4.7 0.0 copy-start
  4.7 1.1 copy-done
  5.8 150.9 %shard_map.68 = (bf16[768,384]{1,0:T(8,128)(2,1)S(1)}, f32[8,128]{1,0:T(8,128)S(1)}) custom-call(s32[90]{0:T(128)S(1)} %concatenate.3.meta, bf16[768,384]{1,0:T(8,128)(2,1)S(1)} %copy-done, f32[18,1,128]{2,1,0:T(1,128)S(1)} %broadcast_in_dim.61.pat), custom_call_target="tpu_custom_call" | custom-call | flops 3623878656 | bytes 1179648 | tf_op jit(solution)/shard_map/pallas_call | solution.py:346
  156.6 0.6 slice_reduce_fusion
  157.3 0.8 copy.15
  (11 shorter events, 0.1 us)
Async XLA Ops:
  0.7 0.7 copy-start.4
  1.4 0.7 copy-start.3
  2.2 0.7 copy-start.1
  3.1 0.7 copy-start.2
  4.7 1.1 copy-start

commit v3 on v2

--- a/solution.py
+++ b/solution.py
@@ -15,9 +15,9 @@
 def kernel(
     nrow, ncol, nrb, ncb, at,
     meta, dens, pat, out, traces,
-    panel_0, panel_1, panel_2, column_0, column_1, column_2, pat_row, pat_col, sum_row, sum_col, acc, diag,
+    panel_0, panel_1, panel_2, column_0, column_1, column_2, pat_row, pat_col, sum_row, sum_col, acc, diag, served, given,
     p_recv, p_up, p_down, p_part, c_recv, c_send,
-    pr_recv, pr_send, pc_recv, pc_send, sr_recv, sr_send, sc_recv, sc_send,
+    pr_recv, pr_send, pc_recv, pc_send, sr_recv, sr_send, sc_recv, sc_send, give_recv, give_send,
 ):
     panel, column = (panel_0, panel_1, panel_2), (column_0, column_1, column_2)
     rows, cols = dens.shape
@@ -58,43 +58,57 @@
     def small_col(buf, send, recv, slot, d):
         return remote(buf.at[slot], send.at[d], recv.at[slot], (r, other_col(d)))
 
-    def begin(ph):
-        @pl.when(g + 1 < groups)
+    inner = (g > 0) & (g + 1 < groups)
+
+    def lanes(ph):
+        end = 1 if ph == 1 else 0
+        return g + 1 < groups - end, g > end, inner if ph == 1 else g >= 0
+
+    def hand_on(ph, slot, up, down, act):
+        if up is not None:
+            @pl.when(up)
+            def _():
+                act(along_col(ph, slot, c + 2, p_up))
+
+        if down is not None:
+            @pl.when(down)
+            def _():
+                act(along_col(ph, slot, c - 2, p_down))
+
+    def start(copy):
+        copy.start()
+
+    def sent(copy):
+        copy.wait_send()
+
+    def begin_col(ph):
+        up, down, any_in = lanes(ph)
+        hand_on(ph, c, up, down, start)
+
+        @pl.when(any_in)
         def _():
-            along_col(ph, c, c + 2, p_up).start()
-
-        @pl.when(g > 0)
-        def _():
-            along_col(ph, c, c - 2, p_down).start()
-
-        along_col(ph, c, partner, p_part).start()
+            along_col(ph, c, partner, p_part).start()
+
+    def begin_row(ph):
         for d in range(1, nrow):
             along_row(ph, r, other_row(d), d).start()
 
+    def relayed(ph, d, act, incoming):
+        up, down, any_in = lanes(ph)
+        for group, inside, to_up, to_down in (
+            (g - d, g - d >= 0, up, None),
+            (g + d, g + d < groups, None, down),
+        ):
+            @pl.when(inside & any_in)
+            def _():
+                slot = 2 * group + parity
+                if incoming:
+                    along_col(ph, slot, partner, p_part).wait_recv()
+                hand_on(ph, slot, to_up, to_down, act)
+                act(along_col(ph, slot, partner, p_part))
+
     def relay(ph, d):
-        below, above = g - d, g + d
-
-        @pl.when(below >= 0)
-        def _():
-            slot = 2 * below + parity
-            along_col(ph, slot, partner, p_part).wait_recv()
-
-            @pl.when(g + 1 < groups)
-            def _():
-                along_col(ph, slot, c + 2, p_up).start()
-
-            along_col(ph, slot, partner, p_part).start()
-
-        @pl.when(above < groups)
-        def _():
-            slot = 2 * above + parity
-            along_col(ph, slot, partner, p_part).wait_recv()
-
-            @pl.when(g > 0)
-            def _():
-                along_col(ph, slot, c - 2, p_down).start()
-
-            along_col(ph, slot, partner, p_part).start()
+        relayed(ph, d, start, True)
 
     def from_partner(ph, group):
         along_col(ph, 2 * group + 1 - parity, partner, p_part).wait_recv()
@@ -104,41 +118,32 @@
             along_row(ph, other_row(d), other_row(1), d).wait_recv()
 
     def finish(ph):
-        along_col(ph, c, partner, p_part).wait_send()
-
-        @pl.when(g + 1 < groups)
+        up, down, any_in = lanes(ph)
+        hand_on(ph, c, up, down, sent)
+
+        @pl.when(any_in)
         def _():
-            along_col(ph, c, c + 2, p_up).wait_send()
-
-        @pl.when(g > 0)
-        def _():
-            along_col(ph, c, c - 2, p_down).wait_send()
+            along_col(ph, c, partner, p_part).wait_send()
 
         for d in range(1, groups):
-            below, above = g - d, g + d
-
-            @pl.when(below >= 0)
-            def _():
-                slot = 2 * below + parity
-
-                @pl.when(g + 1 < groups)
-                def _():
-                    along_col(ph, slot, c + 2, p_up).wait_send()
-
-                along_col(ph, slot, partner, p_part).wait_send()
-
-            @pl.when(above < groups)
-            def _():
-                slot = 2 * above + parity
-
-                @pl.when(g > 0)
-                def _():
-                    along_col(ph, slot, c - 2, p_down).wait_send()
-
-                along_col(ph, slot, partner, p_part).wait_send()
-
+            relayed(ph, d, sent, False)
         for d in range(1, nrow):
             along_row(ph, r, other_row(d), d).wait_send()
+
+    def serve(act):
+        @pl.when(g == groups - 2)
+        def _():
+            act(give(c + 2))
+
+        @pl.when(g == 1)
+        def _():
+            act(give(c - 2))
+
+    def give(to):
+        return pltpu.make_async_remote_copy(
+            src_ref=served, dst_ref=given, send_sem=give_send.at[0], recv_sem=give_recv.at[0],
+            device_id=(r, to), device_id_type=MESH,
+        )
 
     half = rows // 2
 
@@ -201,7 +206,8 @@
             value = dens[block(i, j)] * meta[at["occupied"] + i * ncb + j].astype(F32).astype(BF16)
             panel[0][c, j, pl.ds(i * bdim, bdim), :] = value
             column[0][r, i, :, pl.ds(j * bdim, bdim)] = value
-    begin(0)
+    begin_col(0)
+    begin_row(0)
     pat_row[c] = pat[...]
     pat_col[r] = pat[...]
     for d in range(1, nrow):
@@ -216,7 +222,8 @@
             value = (acc[block(i, j)] * keep).astype(BF16)
             panel[1][c, j, pl.ds(i * bdim, bdim), :] = value
             column[1][r, i, :, pl.ds(j * bdim, bdim)] = value
-    begin(1)
+    begin_row(1)
+    begin_col(1)
     diag[...] = jnp.zeros_like(diag)
     diag[0:1, :] = trace_of(lambda i, j: panel[1][c, j, pl.ds(i * bdim, bdim), :].astype(F32))
 
@@ -224,8 +231,7 @@
         small_col(pat_row, pr_send, pr_recv, other_col(d), 1).wait_recv()
     for d in range(1, nrow):
         small_row(pat_col, pc_send, pc_recv, other_row(d), 1).wait_recv()
-    for d in range(1, groups):
-        relay(1, d)
+    relay(1, 1)
     columns_in(1)
     for i in range(nrb):
         for j in range(ncb):
@@ -236,24 +242,39 @@
             ]
             panel[2][c, j, pl.ds(i * bdim, bdim), :] = value * mask
 
-    def others(k, _):
-        @pl.when(k != g)
+    begin_col(2)
+    for d in range(2, groups):
+        relay(1, d)
+
+    @pl.when(inner)
+    def _():
+        def arrived(k, _):
+            from_partner(1, k)
+            return 0
+
+        lax.fori_loop(0, groups, arrived, 0)
+
+        @pl.when((g == groups - 2) | (g == 1))
         def _():
-            from_partner(1, k)
-
-        return 0
-
-    from_partner(1, g)
-    lax.fori_loop(0, groups, others, 0)
+            for j in range(ncb):
+                served[j] = panel[1][meta[at["serve_dev"] + j], meta[at["serve_local"] + j]]
+
+        serve(start)
+        for j in range(ncb):
+            given[j] = panel[1][meta[at["col_dev"] + j], meta[at["col_local"] + j]]
+
+    @pl.when(jnp.logical_not(inner))
+    def _():
+        give(partner).wait_recv()
+
     for j in range(ncb):
         for i in range(nrb):
             mask = pat_col[
                 meta[at["row_to_dev"] + i], meta[at["row_to_local"] + i] + nrb * j
             ].astype(BF16)
-            value = panel[1][meta[at["col_dev"] + j], meta[at["col_local"] + j], pl.ds(i * bdim, bdim), :
-            ]
+            value = given[j, pl.ds(i * bdim, bdim), :]
             column[2][r, i, :, pl.ds(j * bdim, bdim)] = value * mask
-    begin(2)
+    begin_row(2)
     multiply(2)
     for j in range(ncb):
         for i in range(nrb):
@@ -268,6 +289,7 @@
         small_row(sum_row, sr_send, sr_recv, r, d).start()
     for ph in range(3):
         finish(ph)
+    serve(sent)
     for d in range(1, nrow):
         small_row(sum_row, sr_send, sr_recv, other_row(d), 1).wait_recv()
     sum_col[c] = functools.reduce(lambda a, b: a + b, [sum_row[k] for k in range(nrow)])
@@ -307,6 +329,8 @@
         return jnp.sum(jnp.where(wanted[:, None] == target[None, :], blocks[None, :], 0), axis=1)
 
     source_rows, source_cols = source_of(row_blocks), source_of(col_blocks)
+    serve_col = jnp.where(col_index // 2 == 1, col_index - 2, lax.rem(col_index + 2, ncol))
+    served_cols = source_of(serve_col * ncb + jnp.arange(ncb, dtype=jnp.int32))
     target_rows = lax.dynamic_slice(target, (row_index * nrb,), (nrb,))
     target_cols = lax.dynamic_slice(target, (col_index * ncb,), (ncb,))
     slots = jnp.arange(nrb * ncb, dtype=jnp.int32)
@@ -316,6 +340,8 @@
         "row_local": source_rows % nrb,
         "col_dev": source_cols // ncb,
         "col_local": source_cols % ncb,
+        "serve_dev": served_cols // ncb,
+        "serve_local": served_cols % ncb,
         "row_to_dev": target_rows // nrb,
         "row_to_local": target_rows % nrb,
         "col_to_dev": target_cols // ncb,
@@ -341,6 +367,7 @@
         pltpu.VMEM((ncol, 8, 128), F32),
         pltpu.VMEM((rows, cols), F32),
         pltpu.VMEM((8, 128), F32),
+        *[pltpu.VMEM((ncb, rows, rows // nrb), BF16)] * 2,
     ]
     held = 3 * (nrow + ncol) * rows * cols * 2
     second, sums = pl.pallas_call(
@@ -356,7 +383,8 @@
         + [dma((3, nrow))] * 2
         + [dma((ncol,))] * 2
         + [dma((nrow,))] * 4
-        + [dma((ncol,))] * 2,
+        + [dma((ncol,))] * 2
+        + [dma((1,))] * 2,
         compiler_params=pltpu.CompilerParams(
             collective_id=0, has_side_effects=True, vmem_limit_bytes=held + (10 << 20)
         ),

time: 158 us -> 140 us (0.89)
  Pallas kernels: 151 us -> 133 us
    pallas_call x1, Pallas kernels: 151 us -> 133 us  [body(): pl.pallas_call(functools.partial(kernel, nrow, ncol, nrb, ncb, at), out_s...]
where the time goes in v3:
time: 140 us
  Pallas kernels  133 us (95%)
  local copies, waits for them, and re-layouts  5.7 us (4%)
    pallas_call x1, Pallas kernels, body(): pl.pallas_call(functools.partial(kernel, nrow, ncol, nrb, ncb, at), out_s...  133 us
    unnamed x13, local copies, waits for them, and re-layouts  4.4 us

profile of v3, /device:TPU:0, one launch (start us, length us, event | category | flops | bytes accessed | tf_op | source)
XLA Modules:
  0.0 140.0 jit_solution(17544279852180193281)
XLA Ops:
  0.7 0.0 copy-start.4
  0.7 0.7 copy-done.4
  1.4 0.1 fusion
  1.5 0.0 copy-start.3
  1.5 0.1 reshape.137
  1.6 0.6 copy-done.3
  2.1 0.1 tile.7
  2.2 0.0 copy-start.1
  2.3 0.1 eq.106
  2.4 0.6 copy-done.1
  2.9 0.1 broadcast_in_dim.70
  3.0 0.1 copy.10
  3.1 0.0 copy-start.2
  3.1 0.1 reshape_squeeze.3
  3.2 0.6 copy-done.2
  3.8 0.1 copy.9
  3.9 0.1 select_reduce_fusion
  4.0 0.2 select_reduce_fusion.1
  4.2 0.2 select_reduce_fusion.2
  4.4 0.1 and_select_fusion
  4.5 0.1 and_select_fusion.2
  4.6 0.1 concatenate.3.meta
  4.7 0.1 broadcast_in_dim.71.pat
  4.8 0.0 copy-start
  4.8 1.1 copy-done
  5.9 132.7 %shard_map.68 = (bf16[768,384]{1,0:T(8,128)(2,1)S(1)}, f32[8,128]{1,0:T(8,128)S(1)}) custom-call(s32[96]{0:T(128)S(1)} %concatenate.3.meta, bf16[768,384]{1,0:T(8,128)(2,1)S(1)} %copy-done, f32[18,1,128]{2,1,0:T(1,128)S(1)} %broadcast_in_dim.71.pat), custom_call_target="tpu_custom_call" | custom-call | flops 3623878656 | bytes 1179648 | tf_op jit(solution)/shard_map/pallas_call | solution.py:373
  138.5 0.6 slice_reduce_fusion
  139.2 0.8 copy.15
  (13 shorter events, 0.1 us)
Async XLA Ops:
  0.7 0.7 copy-start.4
  1.5 0.7 copy-start.3
  2.2 0.7 copy-start.1
  3.1 0.7 copy-start.2
  4.8 1.1 copy-start

commit v4 on v3

--- a/solution.py
+++ b/solution.py
@@ -15,11 +15,16 @@
 def kernel(
     nrow, ncol, nrb, ncb, at,
     meta, dens, pat, out, traces,
-    panel_0, panel_1, panel_2, column_0, column_1, column_2, pat_row, pat_col, sum_row, sum_col, acc, diag, served, given,
-    p_recv, p_up, p_down, p_part, c_recv, c_send,
-    pr_recv, pr_send, pc_recv, pc_send, sr_recv, sr_send, sc_recv, sc_send, give_recv, give_send,
+    panel_0, panel_1, panel_2, *rest,
 ):
-    panel, column = (panel_0, panel_1, panel_2), (column_0, column_1, column_2)
+    panel = (panel_0, panel_1, panel_2)
+    column = [rest[ph * ncb : (ph + 1) * ncb] for ph in range(3)]
+    (
+        pat_row, pat_col, sum_row, sum_col, acc, diag, served, given,
+        p_recv, p_up, p_down, p_part, c_recv, c_send,
+        pr_recv, pr_send, pc_recv, pc_send, sr_recv, sr_send, sc_recv, sc_send,
+        give_recv, give_send,
+    ) = rest[3 * ncb :]
     rows, cols = dens.shape
     bdim = rows // nrb
     groups = ncol // 2
@@ -46,11 +51,11 @@
             device_id=device, device_id_type=MESH,
         )
 
-    def along_col(ph, slot, to, sem):
-        return remote(panel[ph].at[slot], sem.at[ph, slot], p_recv.at[ph, slot], (r, to))
-
-    def along_row(ph, slot, to, d):
-        return remote(column[ph].at[slot], c_send.at[ph, d], c_recv.at[ph, slot], (to, c))
+    def along_col(ph, slot, j, to, sem):
+        return remote(panel[ph].at[slot, j], sem.at[ph, slot, j], p_recv.at[ph, slot, j], (r, to))
+
+    def along_row(ph, slot, j, to, d):
+        return remote(column[ph][j].at[slot], c_send.at[ph, d, j], c_recv.at[ph, slot, j], (to, c))
 
     def small_row(buf, send, recv, slot, d):
         return remote(buf.at[slot], send.at[d], recv.at[slot], (other_row(d), c))
@@ -64,16 +69,16 @@
         end = 1 if ph == 1 else 0
         return g + 1 < groups - end, g > end, inner if ph == 1 else g >= 0
 
-    def hand_on(ph, slot, up, down, act):
+    def hand_on(ph, slot, j, up, down, act):
         if up is not None:
             @pl.when(up)
             def _():
-                act(along_col(ph, slot, c + 2, p_up))
+                act(along_col(ph, slot, j, c + 2, p_up))
 
         if down is not None:
             @pl.when(down)
             def _():
-                act(along_col(ph, slot, c - 2, p_down))
+                act(along_col(ph, slot, j, c - 2, p_down))
 
     def start(copy):
         copy.start()
@@ -81,19 +86,19 @@
     def sent(copy):
         copy.wait_send()
 
-    def begin_col(ph):
+    def own_col(ph, j, act):
         up, down, any_in = lanes(ph)
-        hand_on(ph, c, up, down, start)
+        hand_on(ph, c, j, up, down, act)
 
         @pl.when(any_in)
         def _():
-            along_col(ph, c, partner, p_part).start()
-
-    def begin_row(ph):
+            act(along_col(ph, c, j, partner, p_part))
+
+    def own_row(ph, j, act):
         for d in range(1, nrow):
-            along_row(ph, r, other_row(d), d).start()
-
-    def relayed(ph, d, act, incoming):
+            act(along_row(ph, r, j, other_row(d), d))
+
+    def relayed(ph, d, j, act, incoming):
         up, down, any_in = lanes(ph)
         for group, inside, to_up, to_down in (
             (g - d, g - d >= 0, up, None),
@@ -103,45 +108,42 @@
             def _():
                 slot = 2 * group + parity
                 if incoming:
-                    along_col(ph, slot, partner, p_part).wait_recv()
-                hand_on(ph, slot, to_up, to_down, act)
-                act(along_col(ph, slot, partner, p_part))
+                    along_col(ph, slot, j, partner, p_part).wait_recv()
+                hand_on(ph, slot, j, to_up, to_down, act)
+                act(along_col(ph, slot, j, partner, p_part))
 
     def relay(ph, d):
-        relayed(ph, d, start, True)
+        for j in range(ncb):
+            relayed(ph, d, j, start, True)
 
     def from_partner(ph, group):
-        along_col(ph, 2 * group + 1 - parity, partner, p_part).wait_recv()
-
-    def columns_in(ph):
+        for j in range(ncb):
+            along_col(ph, 2 * group + 1 - parity, j, partner, p_part).wait_recv()
+
+    def columns_in(ph, j):
         for d in range(1, nrow):
-            along_row(ph, other_row(d), other_row(1), d).wait_recv()
+            along_row(ph, other_row(d), j, other_row(1), d).wait_recv()
 
     def finish(ph):
-        up, down, any_in = lanes(ph)
-        hand_on(ph, c, up, down, sent)
-
-        @pl.when(any_in)
-        def _():
-            along_col(ph, c, partner, p_part).wait_send()
-
-        for d in range(1, groups):
-            relayed(ph, d, sent, False)
-        for d in range(1, nrow):
-            along_row(ph, r, other_row(d), d).wait_send()
-
-    def serve(act):
+        for j in range(ncb):
+            own_col(ph, j, sent)
+            own_row(ph, j, sent)
+            for d in range(1, groups):
+                relayed(ph, d, j, sent, False)
+
+    def serve(j, act):
         @pl.when(g == groups - 2)
         def _():
-            act(give(c + 2))
+            act(give(j, c + 2))
 
         @pl.when(g == 1)
         def _():
-            act(give(c - 2))
-
-    def give(to):
+            act(give(j, c - 2))
+
+    def give(j, to):
         return pltpu.make_async_remote_copy(
-            src_ref=served, dst_ref=given, send_sem=give_send.at[0], recv_sem=give_recv.at[0],
+            src_ref=served.at[j], dst_ref=given.at[j],
+            send_sem=give_send.at[j], recv_sem=give_recv.at[j],
             device_id=(r, to), device_id_type=MESH,
         )
 
@@ -156,7 +158,10 @@
                 from_partner(ph, group)
 
                 def part(q, _):
-                    right = column[ph][group, pl.ds(q * ncb, ncb)].reshape(cols, cols)
+                    right = jnp.concatenate(
+                        [column[ph][j][group, pl.ds(q * ncb, ncb)].reshape(cols, bdim) for j in range(ncb)],
+                        axis=1,
+                    )
                     for k in range(2):
                         here = pl.ds(k * half, half)
                         left = jnp.concatenate(
@@ -177,7 +182,8 @@
         for d in range(1, groups):
             relay(ph, d)
             if d == first:
-                columns_in(ph)
+                for j in range(ncb):
+                    columns_in(ph, j)
 
                 def early(e, _):
                     compute(ph, e)
@@ -201,13 +207,13 @@
                 total += jnp.where(eye & hit, ref_value(i, j), 0.0)
         return jnp.sum(total, axis=0, keepdims=True)
 
-    for i in range(nrb):
-        for j in range(ncb):
+    for j in range(ncb):
+        for i in range(nrb):
             value = dens[block(i, j)] * meta[at["occupied"] + i * ncb + j].astype(F32).astype(BF16)
             panel[0][c, j, pl.ds(i * bdim, bdim), :] = value
-            column[0][r, i, :, pl.ds(j * bdim, bdim)] = value
-    begin_col(0)
-    begin_row(0)
+            column[0][j][r, i] = value
+        own_col(0, j, start)
+        own_row(0, j, start)
     pat_row[c] = pat[...]
     pat_col[r] = pat[...]
     for d in range(1, nrow):
@@ -216,14 +222,14 @@
         small_col(pat_row, pr_send, pr_recv, c, d).start()
 
     multiply(0)
-    for i in range(nrb):
-        for j in range(ncb):
+    for j in range(ncb):
+        for i in range(nrb):
             keep = meta[at["keep"] + i * ncb + j].astype(F32)
             value = (acc[block(i, j)] * keep).astype(BF16)
             panel[1][c, j, pl.ds(i * bdim, bdim), :] = value
-            column[1][r, i, :, pl.ds(j * bdim, bdim)] = value
-    begin_row(1)
-    begin_col(1)
+            column[1][j][r, i] = value
+        own_row(1, j, start)
+        own_col(1, j, start)
     diag[...] = jnp.zeros_like(diag)
     diag[0:1, :] = trace_of(lambda i, j: panel[1][c, j, pl.ds(i * bdim, bdim), :].astype(F32))
 
@@ -231,18 +237,16 @@
         small_col(pat_row, pr_send, pr_recv, other_col(d), 1).wait_recv()
     for d in range(1, nrow):
         small_row(pat_col, pc_send, pc_recv, other_row(d), 1).wait_recv()
-    relay(1, 1)
-    columns_in(1)
-    for i in range(nrb):
-        for j in range(ncb):
+    for j in range(ncb):
+        relayed(1, 1, j, start, True)
+        columns_in(1, j)
+        for i in range(nrb):
             mask = pat_row[
                 meta[at["col_to_dev"] + j], meta[at["col_to_local"] + j] * nrb + i
             ].astype(BF16)
-            value = column[1][meta[at["row_dev"] + i], meta[at["row_local"] + i], :, pl.ds(j * bdim, bdim)
-            ]
+            value = column[1][j][meta[at["row_dev"] + i], meta[at["row_local"] + i]]
             panel[2][c, j, pl.ds(i * bdim, bdim), :] = value * mask
-
-    begin_col(2)
+        own_col(2, j, start)
     for d in range(2, groups):
         relay(1, d)
 
@@ -258,14 +262,15 @@
         def _():
             for j in range(ncb):
                 served[j] = panel[1][meta[at["serve_dev"] + j], meta[at["serve_local"] + j]]
-
-        serve(start)
+                serve(j, start)
+
         for j in range(ncb):
             given[j] = panel[1][meta[at["col_dev"] + j], meta[at["col_local"] + j]]
 
     @pl.when(jnp.logical_not(inner))
     def _():
-        give(partner).wait_recv()
+        for j in range(ncb):
+            give(j, partner).wait_recv()
 
     for j in range(ncb):
         for i in range(nrb):
@@ -273,8 +278,8 @@
                 meta[at["row_to_dev"] + i], meta[at["row_to_local"] + i] + nrb * j
             ].astype(BF16)
             value = given[j, pl.ds(i * bdim, bdim), :]
-            column[2][r, i, :, pl.ds(j * bdim, bdim)] = value * mask
-    begin_row(2)
+            column[2][j][r, i] = value * mask
+        own_row(2, j, start)
     multiply(2)
     for j in range(ncb):
         for i in range(nrb):
@@ -289,7 +294,12 @@
         small_row(sum_row, sr_send, sr_recv, r, d).start()
     for ph in range(3):
         finish(ph)
-    serve(sent)
+
+    @pl.when((g == groups - 2) | (g == 1))
+    def _():
+        for j in range(ncb):
+            serve(j, sent)
+
     for d in range(1, nrow):
         small_row(sum_row, sr_send, sr_recv, other_row(d), 1).wait_recv()
     sum_col[c] = functools.reduce(lambda a, b: a + b, [sum_row[k] for k in range(nrow)])
@@ -360,7 +370,7 @@
     vmem = pl.BlockSpec(memory_space=pltpu.VMEM)
     scratch = [
         *[pltpu.VMEM((ncol, ncb, rows, rows // nrb), BF16)] * 3,
-        *[pltpu.VMEM((nrow, nrb, rows // nrb, cols), BF16)] * 3,
+        *[pltpu.VMEM((nrow, nrb, rows // nrb, rows // nrb), BF16)] * (3 * ncb),
         pltpu.VMEM((ncol, ncb * nrb, 1, 128), F32),
         pltpu.VMEM((nrow, ncb * nrb, 1, 128), F32),
         pltpu.VMEM((nrow, 8, 128), F32),
@@ -379,12 +389,12 @@
         in_specs=[pl.BlockSpec(memory_space=pltpu.SMEM), vmem, vmem],
         out_specs=(vmem, vmem),
         scratch_shapes=scratch
-        + [dma((3, ncol))] * 4
-        + [dma((3, nrow))] * 2
+        + [dma((3, ncol, ncb))] * 4
+        + [dma((3, nrow, ncb))] * 2
         + [dma((ncol,))] * 2
         + [dma((nrow,))] * 4
         + [dma((ncol,))] * 2
-        + [dma((1,))] * 2,
+        + [dma((ncb,))] * 2,
         compiler_params=pltpu.CompilerParams(
             collective_id=0, has_side_effects=True, vmem_limit_bytes=held + (10 << 20)
         ),

time: 140 us -> 146 us (1.043)
  Pallas kernels: 133 us -> 139 us
    pallas_call x1, Pallas kernels: 133 us -> 139 us  [body(): pl.pallas_call(functools.partial(kernel, nrow, ncol, nrb, ncb, at), out_s...]
where the time goes in v4:
time: 146 us
  Pallas kernels  139 us (95%)
  local copies, waits for them, and re-layouts  5.7 us (4%)
    pallas_call x1, Pallas kernels, body(): pl.pallas_call(functools.partial(kernel, nrow, ncol, nrb, ncb, at), out_s...  139 us
    unnamed x13, local copies, waits for them, and re-layouts  4.4 us

profile of v4, /device:TPU:0, one launch (start us, length us, event | category | flops | bytes accessed | tf_op | source)
XLA Modules:
  0.0 145.9 jit_solution(5841812837299523923)
XLA Ops:
  0.7 0.0 copy-start.4
  0.7 0.7 copy-done.4
  1.4 0.1 fusion
  1.5 0.0 copy-start.3
  1.5 0.1 reshape.137
  1.6 0.6 copy-done.3
  2.1 0.1 tile.7
  2.2 0.0 copy-start.1
  2.3 0.1 eq.106
  2.4 0.6 copy-done.1
  2.9 0.1 broadcast_in_dim.70
  3.0 0.1 copy.10
  3.1 0.0 copy-start.2
  3.1 0.1 reshape_squeeze.3
  3.2 0.6 copy-done.2
  3.8 0.1 copy.9
  3.9 0.1 select_reduce_fusion
  4.0 0.2 select_reduce_fusion.1
  4.2 0.2 select_reduce_fusion.2
  4.4 0.1 and_select_fusion
  4.5 0.1 and_select_fusion.2
  4.6 0.1 concatenate.3.meta
  4.7 0.1 broadcast_in_dim.71.pat
  4.8 0.0 copy-start
  4.8 1.1 copy-done
  5.9 138.6 %shard_map.68 = (bf16[768,384]{1,0:T(8,128)(2,1)S(1)}, f32[8,128]{1,0:T(8,128)S(1)}) custom-call(s32[96]{0:T(128)S(1)} %concatenate.3.meta, bf16[768,384]{1,0:T(8,128)(2,1)S(1)} %copy-done, f32[18,1,128]{2,1,0:T(1,128)S(1)} %broadcast_in_dim.71.pat), custom_call_target="tpu_custom_call" | custom-call | flops 3623878656 | bytes 1179648 | tf_op jit(solution)/shard_map/pallas_call | solution.py:383
  144.4 0.6 slice_reduce_fusion
  145.0 0.8 copy.15
  (13 shorter events, 0.1 us)
Async XLA Ops:
  0.7 0.7 copy-start.4
  1.5 0.7 copy-start.3
  2.2 0.7 copy-start.1
  3.1 0.7 copy-start.2
  4.8 1.1 copy-start

commit v5 on v4

--- a/solution.py
+++ b/solution.py
@@ -237,8 +237,8 @@
         small_col(pat_row, pr_send, pr_recv, other_col(d), 1).wait_recv()
     for d in range(1, nrow):
         small_row(pat_col, pc_send, pc_recv, other_row(d), 1).wait_recv()
+    relay(1, 1)
     for j in range(ncb):
-        relayed(1, 1, j, start, True)
         columns_in(1, j)
         for i in range(nrb):
             mask = pat_row[

time: 146 us -> 141 us (0.966)
  Pallas kernels: 139 us -> 134 us
    pallas_call x1, Pallas kernels: 139 us -> 134 us  [body(): pl.pallas_call(functools.partial(kernel, nrow, ncol, nrb, ncb, at), out_s...]
where the time goes in v5:
time: 141 us
  Pallas kernels  134 us (95%)
  local copies, waits for them, and re-layouts  5.7 us (4%)
    pallas_call x1, Pallas kernels, body(): pl.pallas_call(functools.partial(kernel, nrow, ncol, nrb, ncb, at), out_s...  134 us
    unnamed x13, local copies, waits for them, and re-layouts  4.4 us

profile of v5, /device:TPU:0, one launch (start us, length us, event | category | flops | bytes accessed | tf_op | source)
XLA Modules:
  0.0 141.1 jit_solution(2172789870946608924)
XLA Ops:
  0.7 0.0 copy-start.4
  0.7 0.7 copy-done.4
  1.4 0.1 fusion
  1.5 0.0 copy-start.3
  1.5 0.1 reshape.137
  1.6 0.6 copy-done.3
  2.1 0.1 tile.7
  2.2 0.0 copy-start.1
  2.3 0.1 eq.106
  2.4 0.6 copy-done.1
  2.9 0.1 broadcast_in_dim.70
  3.0 0.1 copy.10
  3.1 0.0 copy-start.2
  3.1 0.1 reshape_squeeze.3
  3.2 0.6 copy-done.2
  3.8 0.1 copy.9
  3.9 0.1 select_reduce_fusion
  4.0 0.2 select_reduce_fusion.1
  4.2 0.2 select_reduce_fusion.2
  4.4 0.1 and_select_fusion
  4.5 0.1 and_select_fusion.2
  4.6 0.1 concatenate.3.meta
  4.7 0.1 broadcast_in_dim.71.pat
  4.8 0.0 copy-start
  4.8 1.1 copy-done
  5.9 133.8 %shard_map.68 = (bf16[768,384]{1,0:T(8,128)(2,1)S(1)}, f32[8,128]{1,0:T(8,128)S(1)}) custom-call(s32[96]{0:T(128)S(1)} %concatenate.3.meta, bf16[768,384]{1,0:T(8,128)(2,1)S(1)} %copy-done, f32[18,1,128]{2,1,0:T(1,128)S(1)} %broadcast_in_dim.71.pat), custom_call_target="tpu_custom_call" | custom-call | flops 3623878656 | bytes 1179648 | tf_op jit(solution)/shard_map/pallas_call | solution.py:383
  139.7 0.6 slice_reduce_fusion
  140.3 0.8 copy.15
  (13 shorter events, 0.1 us)
Async XLA Ops:
  0.7 0.7 copy-start.4
  1.5 0.7 copy-start.3
  2.2 0.7 copy-start.1
  3.1 0.7 copy-start.2
  4.8 1.1 copy-start

commit v6 on v5

--- a/solution.py
+++ b/solution.py
@@ -228,7 +228,8 @@
             value = (acc[block(i, j)] * keep).astype(BF16)
             panel[1][c, j, pl.ds(i * bdim, bdim), :] = value
             column[1][j][r, i] = value
-        own_row(1, j, start)
+        if j + 1 < ncb:
+            own_row(1, j, start)
         own_col(1, j, start)
     diag[...] = jnp.zeros_like(diag)
     diag[0:1, :] = trace_of(lambda i, j: panel[1][c, j, pl.ds(i * bdim, bdim), :].astype(F32))
@@ -238,6 +239,7 @@
     for d in range(1, nrow):
         small_row(pat_col, pc_send, pc_recv, other_row(d), 1).wait_recv()
     relay(1, 1)
+    own_row(1, ncb - 1, start)
     for j in range(ncb):
         columns_in(1, j)
         for i in range(nrb):

time: 141 us -> 143 us (1.014)
  no operation moved by 1% of the time
where the time goes in v6:
time: 143 us
  Pallas kernels  135 us (94%)
  local copies, waits for them, and re-layouts  5.7 us (4%)
    pallas_call x1, Pallas kernels, body(): pl.pallas_call(functools.partial(kernel, nrow, ncol, nrb, ncb, at), out_s...  135 us
    unnamed x13, local copies, waits for them, and re-layouts  4.4 us

profile of v6, /device:TPU:0, one launch (start us, length us, event | category | flops | bytes accessed | tf_op | source)
XLA Modules:
  0.0 142.5 jit_solution(11573895763308650472)
XLA Ops:
  0.7 0.0 copy-start.4
  0.7 0.7 copy-done.4
  1.4 0.1 fusion
  1.5 0.0 copy-start.3
  1.5 0.1 reshape.137
  1.6 0.6 copy-done.3
  2.1 0.1 tile.7
  2.2 0.0 copy-start.1
  2.3 0.1 eq.106
  2.4 0.6 copy-done.1
  2.9 0.1 broadcast_in_dim.70
  3.0 0.1 copy.10
  3.1 0.0 copy-start.2
  3.1 0.1 reshape_squeeze.3
  3.2 0.6 copy-done.2
  3.8 0.1 copy.9
  3.9 0.1 select_reduce_fusion
  4.0 0.2 select_reduce_fusion.1
  4.2 0.2 select_reduce_fusion.2
  4.4 0.1 and_select_fusion
  4.5 0.1 and_select_fusion.2
  4.6 0.1 concatenate.3.meta
  4.7 0.1 broadcast_in_dim.71.pat
  4.8 0.0 copy-start
  4.8 1.1 copy-done
  5.9 135.2 %shard_map.68 = (bf16[768,384]{1,0:T(8,128)(2,1)S(1)}, f32[8,128]{1,0:T(8,128)S(1)}) custom-call(s32[96]{0:T(128)S(1)} %concatenate.3.meta, bf16[768,384]{1,0:T(8,128)(2,1)S(1)} %copy-done, f32[18,1,128]{2,1,0:T(1,128)S(1)} %broadcast_in_dim.71.pat), custom_call_target="tpu_custom_call" | custom-call | flops 3623878656 | bytes 1179648 | tf_op jit(solution)/shard_map/pallas_call | solution.py:385
  141.1 0.6 slice_reduce_fusion
  141.7 0.8 copy.15
  (13 shorter events, 0.1 us)
Async XLA Ops:
  0.7 0.7 copy-start.4
  1.5 0.7 copy-start.3
  2.2 0.7 copy-start.1
  3.1 0.7 copy-start.2
  4.8 1.1 copy-start
